TPU v7x, 512 devices: a whole 4x8x8 slice. The times are simulated.
512 devices in a mesh: dp: 8 (over z_lo, core), ctx: 64 (over z_hi, y, x).
Axes of the slice: x: 4, y: 8, z: 8 (z_hi: 2, z_lo: 4; z = z_hi * 4 + z_lo), core: 2. Of those that a mesh axis runs over, the one named last changes fastest.
Arguments:
- query_gate: bfloat16 [8, 512, 8192], P('dp', None, 'ctx'), may hold values from -6 to 6
- key_gate: bfloat16 [8, 512, 8192], P('dp', None, 'ctx'), may hold values from -6 to 6
- value_gate: bfloat16 [8, 512, 8192], P('dp', None, 'ctx'), may hold values from -6 to 6
- grad_out: bfloat16 [8, 512, 8192], P('dp', None, 'ctx'), may hold values from -6 to 6
- long_filter: float32 [512, 8192], P('ctx'), may hold values from -1 to 1
Outputs:
- grad_query: bfloat16 [8, 512, 8192], P('dp', None, 'ctx')
- grad_key: bfloat16 [8, 512, 8192], P('dp', None, 'ctx')
- grad_value: bfloat16 [8, 512, 8192], P('dp', None, 'ctx')
- grad_filter: float32 [512, 8192], P('ctx', 'dp')
All inputs are finite; a program needn't handle non-finite values.
Results may differ from a plain program's by a relative error of at most 0.017.
Values may be sent and summed in bfloat16 or wider, within the bound.
No kernel may reach another device: no remote copies, remote signals or barrier semaphores. Data moves between devices by JAX's collectives and lax.ppermute only.
A program may use at most 64 MiB of HBM per device.

v0:
```python
import math

import jax
import jax.numpy as jnp
import numpy as np
from jax import lax
from jax.experimental import pallas as pl
from jax.experimental.pallas import tpu as pltpu
from jax.sharding import PartitionSpec as P

BLOCK = 128
bf16 = jnp.bfloat16
f32 = jnp.float32


def split_table(table):
    high = table.astype(bf16)
    return high, (table - high.astype(np.float64)).astype(bf16)


def make_tables(half, seq):
    length = 2 * seq
    k = np.arange(half) + 0.5
    first = 2.0 * math.pi * np.outer(k, np.arange(half)) / (2 * half)
    turn = 2.0 * math.pi * np.outer(k, np.arange(BLOCK)) / length
    block = 2.0 * math.pi * np.outer(np.arange(BLOCK), np.arange(BLOCK)) / BLOCK
    first_high, first_low = split_table(np.concatenate([np.cos(first), -np.sin(first)], 0))
    last_high, last_low = split_table(
        np.concatenate([np.cos(first).T, -np.sin(first).T], 1) * (2.0 / length)
    )
    cos, sin = np.cos(block), np.sin(block)
    mid_high, mid_low = split_table(np.block([[cos, -sin], [sin, cos]]))
    return {
        "forward": np.concatenate([first_high, first_high, first_low], 1),
        "back": np.concatenate([last_high, last_high, last_low], 1),
        "middle": np.concatenate([mid_high, mid_high, mid_low], 0),
        "turn": np.stack([np.cos(turn), np.sin(turn)]).astype(np.float32),
    }


def split(value):
    high = value.astype(bf16)
    return high, (value - high.astype(f32)).astype(bf16)


def dot(left, right):
    return jnp.dot(left, right, preferred_element_type=f32)


def middle_transform(rows, middle_ref):
    high, low = split(rows)
    return dot(jnp.concatenate([high, low, high], 1), middle_ref[...])


def forward_rows(rows_ref, chans, half, exact, forward_ref, turn_ref, middle_ref):
    cols = jnp.concatenate([rows_ref[pl.ds(c, half, stride=chans), :] for c in range(chans)], 1)
    if exact:
        high = cols.astype(bf16)
        table = jnp.concatenate([forward_ref[:, :half], forward_ref[:, 2 * half :]], 1)
        section = dot(table, jnp.concatenate([high, high], 0))
    else:
        high, low = split(cols)
        section = dot(forward_ref[...], jnp.concatenate([high, low, high], 0))
    cos, sin = turn_ref[0], turn_ref[1]
    rows = []
    for c in range(chans):
        re = section[:half, c * BLOCK : (c + 1) * BLOCK]
        im = section[half:, c * BLOCK : (c + 1) * BLOCK]
        rows.append(jnp.concatenate([re * cos + im * sin, im * cos - re * sin], 1))
    return middle_transform(jnp.concatenate(rows, 0), middle_ref)


def inverse_rows(spec, chans, half, out_ref, back_ref, turn_ref, middle_ref):
    inner = middle_transform(spec, middle_ref)
    cos, sin = turn_ref[0], turn_ref[1]
    cols = []
    for c in range(chans):
        re = inner[c * half : (c + 1) * half, :BLOCK]
        minus = inner[c * half : (c + 1) * half, BLOCK:]
        cols.append(jnp.concatenate([re * cos + minus * sin, re * sin - minus * cos], 0))
    high, low = split(jnp.concatenate(cols, 1))
    signal = dot(back_ref[...], jnp.concatenate([high, low, high], 0))
    for c in range(chans):
        out_ref[pl.ds(c, half, stride=chans), :] = signal[:, c * BLOCK : (c + 1) * BLOCK]


def gate_kernel(key_ref, value_ref, grad_ref, query_ref, out_ref):
    groups, both, _ = out_ref.shape
    shape = (groups, both // 2, BLOCK)
    kv = key_ref[...].astype(f32) * value_ref[...].astype(f32)
    dz = grad_ref[...].astype(f32) * query_ref[...].astype(f32)
    out_ref[...] = jnp.concatenate([kv.reshape(shape), dz.reshape(shape)], 1).astype(bf16)


def filter_kernel(filter_ref, forward_ref, turn_ref, middle_ref, spec_ref, rows):
    chans, seq = filter_ref.shape
    half = seq // BLOCK
    for a in range(half):
        rows[pl.ds(a * chans, chans), :] = filter_ref[:, a * BLOCK : (a + 1) * BLOCK]
    spec_ref[...] = forward_rows(rows, chans, half, False, forward_ref, turn_ref, middle_ref)


def forward_kernel(
    both_ref, forward_ref, back_ref, turn_ref, middle_ref, spec_ref, lag_ref, rows, out_rows
):
    half, both, _ = both_ref.shape
    chans = both // 2
    rows[...] = both_ref[...].astype(f32).reshape(half * both, BLOCK)
    spec = forward_rows(rows, both, half, True, forward_ref, turn_ref, middle_ref)
    spec_ref[...] = spec
    count = chans * half
    kv_re, kv_im = spec[:count, :BLOCK], spec[:count, BLOCK:]
    dz_re, dz_im = spec[count:, :BLOCK], spec[count:, BLOCK:]
    cross = jnp.concatenate([kv_re * dz_re + kv_im * dz_im, kv_im * dz_re - kv_re * dz_im], 1)
    inverse_rows(cross, chans, half, out_rows, back_ref, turn_ref, middle_ref)
    lag_ref[...] = out_rows[...].reshape(half, chans, BLOCK).astype(bf16)


def conv_kernel(spec_ref, filter_ref, back_ref, turn_ref, middle_ref, out_ref, out_rows):
    half, both, _ = out_ref.shape
    count = half * both // 2
    f_re, f_im = filter_ref[:, :BLOCK], filter_ref[:, BLOCK:]
    kv_re, kv_im = spec_ref[:count, :BLOCK], spec_ref[:count, BLOCK:]
    dz_re, dz_im = spec_ref[count:, :BLOCK], spec_ref[count:, BLOCK:]
    conv = jnp.concatenate([f_re * kv_re - f_im * kv_im, -f_re * kv_im - f_im * kv_re], 1)
    dkv = jnp.concatenate([f_re * dz_re + f_im * dz_im, f_im * dz_re - f_re * dz_im], 1)
    inverse_rows(
        jnp.concatenate([conv, dkv], 0), both, half, out_rows, back_ref, turn_ref, middle_ref
    )
    out_ref[...] = out_rows[...].reshape(half, both, BLOCK).astype(bf16)


def final_kernel(both_ref, key_ref, value_ref, grad_ref, gq_ref, gk_ref, gv_ref):
    groups, both, _ = both_ref.shape
    chans = both // 2
    wide = both_ref[...].astype(f32)
    conv = wide[:, :chans, :].reshape(groups * chans, BLOCK)
    dkv = wide[:, chans:, :].reshape(groups * chans, BLOCK)
    gq_ref[...] = (grad_ref[...].astype(f32) * conv).astype(bf16)
    gk_ref[...] = (dkv * value_ref[...].astype(f32)).astype(bf16)
    gv_ref[...] = (dkv * key_ref[...].astype(f32)).astype(bf16)


def lag_kernel(terms_ref, out_ref, *, scale):
    wide = terms_ref[...].astype(f32)
    total = wide[0]
    for g in range(1, wide.shape[0]):
        total = total + wide[g]
    total = total * scale
    for a in range(total.shape[0]):
        out_ref[:, a * BLOCK : (a + 1) * BLOCK] = total[a]


def call(kernel, out, *args, scratch=(), flops=0, name=None):
    nbytes = sum(math.prod(a.shape) * a.dtype.itemsize for a in args)
    vmem = pl.BlockSpec(memory_space=pltpu.VMEM)
    return pl.pallas_call(
        kernel,
        out_shape=out,
        in_specs=[vmem] * len(args),
        out_specs=jax.tree.map(lambda _: vmem, out),
        scratch_shapes=[pltpu.VMEM(shape, f32) for shape in scratch],
        compiler_params=pltpu.CompilerParams(vmem_limit_bytes=40 * 2**20),
        cost_estimate=pl.CostEstimate(flops=flops, bytes_accessed=nbytes, transcendentals=0),
        name=name,
    )(*args)


def local(query_gate, key_gate, value_gate, grad_out, long_filter):
    chans, seq = long_filter.shape
    half = seq // BLOCK
    groups = lax.axis_size("dp")
    total = query_gate.shape[1]
    both = 2 * chans
    tables = {name: jnp.asarray(table) for name, table in make_tables(half, seq).items()}
    forward, back = tables["forward"], tables["back"]
    turn, middle = tables["turn"], tables["middle"]
    query, key, value, grad = (
        x.reshape(total, BLOCK) for x in (query_gate, key_gate, value_gate, grad_out)
    )
    shape = jax.ShapeDtypeStruct
    pieces = shape((half, both, BLOCK), bf16)
    work = 2 * chans * half * 256 * 768

    gated = call(gate_kernel, pieces, key, value, grad, query, name="gate")
    here = lax.all_to_all(gated, "ctx", 0, 0, tiled=True)
    filter_spec = call(
        filter_kernel,
        shape((chans * half, 2 * BLOCK), f32),
        long_filter,
        forward,
        turn,
        middle,
        scratch=[(half * chans, BLOCK)],
        flops=2 * work,
        name="filter",
    )
    spec, lag = call(
        forward_kernel,
        (shape((both * half, 2 * BLOCK), f32), shape((half, chans, BLOCK), bf16)),
        here,
        forward,
        back,
        turn,
        middle,
        scratch=[(half * both, BLOCK), (half * chans, BLOCK)],
        flops=4 * work,
        name="forward",
    )
    terms = lax.all_to_all(lag, "dp", 0, 0, tiled=True)
    carried = call(
        conv_kernel,
        pieces,
        spec,
        filter_spec,
        back,
        turn,
        middle,
        scratch=[(half * both, BLOCK)],
        flops=4 * work,
        name="conv",
    )
    back_here = lax.all_to_all(carried, "ctx", 0, 0, tiled=True)
    own = half // groups
    grad_filter = call(
        lambda *refs: lag_kernel(*refs, scale=1.0 / math.sqrt(seq * groups)),
        shape((chans, own * BLOCK), f32),
        terms.reshape(groups, own, chans, BLOCK),
        name="lag_sum",
    )
    grads = call(
        final_kernel,
        (shape((total, BLOCK), bf16),) * 3,
        back_here,
        key,
        value,
        grad,
        name="final",
    )
    return tuple(g[None] for g in grads) + (grad_filter,)


def solution(mesh):
    in_specs = (
        P("dp", None, "ctx"),
        P("dp", None, "ctx"),
        P("dp", None, "ctx"),
        P("dp", None, "ctx"),
        P("ctx", None),
    )
    out_specs = (P("dp", None, "ctx"), P("dp", None, "ctx"), P("dp", None, "ctx"), P("ctx", "dp"))
    return jax.shard_map(local, mesh=mesh, in_specs=in_specs, out_specs=out_specs, check_vma=False)
```

profile of v0, /device:TPU:8, one launch (start us, length us, event | category | flops | bytes accessed | tf_op | source)
XLA Modules:
  0.0 76.9 jit_solution(18323293782900560811)
XLA Ops:
  0.6 0.0 copy-start
  0.6 0.9 %copy-done = bf16[1,512,128]{2,1,0:T(8,128)(2,1)S(1)} copy-done((bf16[1,512,128]{2,1,0:T(8,128)(2,1)S(1)}, bf16[1,512,128]{2,1,0:T(8,128)(2,1)}, u32[]{:S(2)}) %copy-start) | copy-done | bytes 131096
  1.5 0.0 copy-start.2
  1.5 0.9 %copy-done.2 = bf16[1,512,128]{2,1,0:T(8,128)(2,1)S(1)} copy-done((bf16[1,512,128]{2,1,0:T(8,128)(2,1)S(1)}, bf16[1,512,128]{2,1,0:T(8,128)(2,1)}, u32[]{:S(2)}) %copy-start.2) | copy-done | bytes 131096
  2.4 0.0 copy-start.4
  2.4 0.9 %copy-done.4 = bf16[1,512,128]{2,1,0:T(8,128)(2,1)S(1)} copy-done((bf16[1,512,128]{2,1,0:T(8,128)(2,1)S(1)}, bf16[1,512,128]{2,1,0:T(8,128)(2,1)}, u32[]{:S(2)}) %copy-start.4) | copy-done | bytes 131096
  3.3 0.0 copy-start.6
  3.3 0.9 %copy-done.6 = bf16[1,512,128]{2,1,0:T(8,128)(2,1)S(1)} copy-done((bf16[1,512,128]{2,1,0:T(8,128)(2,1)S(1)}, bf16[1,512,128]{2,1,0:T(8,128)(2,1)}, u32[]{:S(2)}) %copy-start.6) | copy-done | bytes 131096
  4.3 0.0 copy-start.11
  4.3 0.1 gate.1
  4.3 0.0 copy-start.8
  4.3 0.0 copy-start.9
  4.3 0.0 copy-start.10
  4.4 36.0 %all_to_all.15.both_ref = bf16[64,16,128]{2,1,0:T(8,128)(2,1)S(1)} all-to-all(bf16[64,16,128]{2,1,0:T(8,128)(2,1)S(1)} %gate.1), channel_id=1, replica_groups=mesh['dp'=8,'ctx'=64] {'ctx'}, dimensions={0} | all-to-all | bytes 524288 | tf_op jit(solution)/shard_map/all_to_all | solution.py:186
  40.3 0.0 copy-done.11
  40.3 0.0 copy-done.8
  40.3 0.0 copy-done.9
  40.4 0.0 copy-done.10
  40.4 2.4 %forward.1 = (f32[1024,256]{1,0:T(8,128)S(1)}, bf16[64,8,128]{2,1,0:T(8,128)(2,1)}) custom-call(bf16[64,16,128]{2,1,0:T(8,128)(2,1)S(1)} %all_to_all.15.both_ref, bf16[128,192]{1,0:T(8,128)(2,1)S(1)} %copy-done.10, bf16[64,384]{1,0:T(8,128)(2,1)S(1)} %copy-done.11, f32[2,64,128]{2,1,0:T(8,128)S(1)} %copy-done.9, bf16[768,256]{1,0:T(8,128)(2,1)S(1)} %copy-done.8), custom_call_target="tpu_custom_call" | custom-call | flops 805306368 | bytes 819200 | tf_op jit(solution)/shard_map/forward/pallas_call | solution.py:157
  42.8 0.0 copy-start.7
  42.8 4.7 %all-to-all-start.2 = ((bf16[64,8,128]{2,1,0:T(8,128)(2,1)}), bf16[64,8,128]{2,1,0:T(8,128)(2,1)S(1)}, u32[]{:S(2)}, u32[]{:S(2)}) async-start(bf16[64,8,128]{2,1,0:T(8,128)(2,1)} %get-tuple-element.13), calls=%async_computation.2 | async-start | bytes 262144 | tf_op jit(solution)/shard_map/all_to_all | solution.py:210
  47.4 0.0 copy-done.7
  47.4 0.6 filter.1.filter_ref
  48.0 1.8 %conv.1 = bf16[64,16,128]{2,1,0:T(8,128)(2,1)} custom-call(f32[1024,256]{1,0:T(8,128)S(1)} %get-tuple-element.9.spec_ref, f32[512,256]{1,0:T(8,128)S(1)} %filter.1.filter_ref, bf16[64,384]{1,0:T(8,128)(2,1)S(1)} %copy-done.11, f32[2,64,128]{2,1,0:T(8,128)S(1)} %copy-done.9, bf16[768,256]{1,0:T(8,128)(2,1)S(1)} %copy-done.8), custom_call_target="tpu_custom_call" | custom-call | flops 805306368 | bytes 2080768 | tf_op jit(solution)/shard_map/conv/pallas_call | solution.py:157
  49.8 4.4 %all-to-all-done.2 = bf16[64,8,128]{2,1,0:T(8,128)(2,1)S(1)} async-done(((bf16[64,8,128]{2,1,0:T(8,128)(2,1)}), bf16[64,8,128]{2,1,0:T(8,128)(2,1)S(1)}, u32[]{:S(2)}, u32[]{:S(2)}) %all-to-all-start.2) | async-done | bytes 131104 | tf_op jit(solution)/shard_map/all_to_all | solution.py:210
  54.2 0.0 copy-start.3
  54.2 0.0 copy-start.5
  54.2 5.0 %all-to-all-start.1 = ((bf16[64,16,128]{2,1,0:T(8,128)(2,1)}), bf16[64,16,128]{2,1,0:T(8,128)(2,1)S(1)}, u32[]{:S(2)}, u32[]{:S(2)}) async-start(bf16[64,16,128]{2,1,0:T(8,128)(2,1)} %conv.1), calls=%async_computation.1 | async-start | bytes 524288 | tf_op jit(solution)/shard_map/all_to_all | solution.py:223
  59.3 0.0 copy-start.1
  59.3 0.6 lag_sum.1
  59.9 16.2 %all-to-all-done.1.both_ref = bf16[64,16,128]{2,1,0:T(8,128)(2,1)S(1)} async-done(((bf16[64,16,128]{2,1,0:T(8,128)(2,1)}), bf16[64,16,128]{2,1,0:T(8,128)(2,1)S(1)}, u32[]{:S(2)}, u32[]{:S(2)}) %all-to-all-start.1) | async-done | bytes 262176 | tf_op jit(solution)/shard_map/all_to_all | solution.py:223
  76.1 0.0 copy-done.3
  76.1 0.0 copy-done.5
  76.1 0.0 copy-done.1
  76.1 0.8 %final.1 = (bf16[512,128]{1,0:T(8,128)(2,1)}, bf16[512,128]{1,0:T(8,128)(2,1)}, bf16[512,128]{1,0:T(8,128)(2,1)}) custom-call(bf16[64,16,128]{2,1,0:T(8,128)(2,1)S(1)} %all-to-all-done.1.both_ref, bf16[512,128]{1,0:T(8,128)(2,1)S(1)} %bitcast.10, bf16[512,128]{1,0:T(8,128)(2,1)S(1)} %bitcast.12, bf16[512,128]{1,0:T(8,128)(2,1)S(1)} %bitcast.14), custom_call_target="tpu_custom_call" | custom-call | bytes 655360 | tf_op jit(solution)/shard_map/final/pallas_call | solution.py:157
Async XLA Ops:
  0.6 0.9 %copy-start = (bf16[1,512,128]{2,1,0:T(8,128)(2,1)S(1)}, bf16[1,512,128]{2,1,0:T(8,128)(2,1)}, u32[]{:S(2)}) copy-start(bf16[1,512,128]{2,1,0:T(8,128)(2,1)} %param.10) | copy-start | bytes 393220
  1.5 0.9 %copy-start.2 = (bf16[1,512,128]{2,1,0:T(8,128)(2,1)S(1)}, bf16[1,512,128]{2,1,0:T(8,128)(2,1)}, u32[]{:S(2)}) copy-start(bf16[1,512,128]{2,1,0:T(8,128)(2,1)} %param.11) | copy-start | bytes 393220
  2.4 0.9 %copy-start.4 = (bf16[1,512,128]{2,1,0:T(8,128)(2,1)S(1)}, bf16[1,512,128]{2,1,0:T(8,128)(2,1)}, u32[]{:S(2)}) copy-start(bf16[1,512,128]{2,1,0:T(8,128)(2,1)} %param.12) | copy-start | bytes 393220
  3.3 0.9 %copy-start.6 = (bf16[1,512,128]{2,1,0:T(8,128)(2,1)S(1)}, bf16[1,512,128]{2,1,0:T(8,128)(2,1)}, u32[]{:S(2)}) copy-start(bf16[1,512,128]{2,1,0:T(8,128)(2,1)} %param.9) | copy-start | bytes 393220
  4.3 36.1 %copy-start.11 = (bf16[64,384]{1,0:T(8,128)(2,1)S(1)}, bf16[64,384]{1,0:T(8,128)(2,1)}, u32[]{:S(2)}) copy-start(bf16[64,384]{1,0:T(8,128)(2,1)} %constant.9.clone.back_ref) | copy-start | bytes 147460
  4.3 36.0 %copy-start.8 = (bf16[768,256]{1,0:T(8,128)(2,1)S(1)}, bf16[768,256]{1,0:T(8,128)(2,1)}, u32[]{:S(2)}) copy-start(bf16[768,256]{1,0:T(8,128)(2,1)} %constant.10.clone.middle_ref) | copy-start | bytes 1179652
  4.3 36.0 %copy-start.9 = (f32[2,64,128]{2,1,0:T(8,128)S(1)}, f32[2,64,128]{2,1,0:T(8,128)}, u32[]{:S(2)}) copy-start(f32[2,64,128]{2,1,0:T(8,128)} %constant.11.clone.turn_ref) | copy-start | bytes 196612
  4.3 36.0 %copy-start.10 = (bf16[128,192]{1,0:T(8,128)(2,1)S(1)}, bf16[128,192]{1,0:T(8,128)(2,1)}, u32[]{:S(2)}) copy-start(bf16[128,192]{1,0:T(8,128)(2,1)} %constant.8.clone.forward_ref) | copy-start | bytes 147460
  42.8 4.7 %copy-start.7 = (f32[8,8192]{1,0:T(8,128)S(1)}, f32[8,8192]{1,0:T(8,128)}, u32[]{:S(2)}) copy-start(f32[8,8192]{1,0:T(8,128)} %filter_ref.1) | copy-start | bytes 786436
  42.8 11.5 %all-to-all-start.2 = ((bf16[64,8,128]{2,1,0:T(8,128)(2,1)}), bf16[64,8,128]{2,1,0:T(8,128)(2,1)S(1)}, u32[]{:S(2)}, u32[]{:S(2)}) async-start(bf16[64,8,128]{2,1,0:T(8,128)(2,1)} %get-tuple-element.13), calls=%async_computation.2 | async-start | bytes 262144 | tf_op jit(solution)/shard_map/all_to_all | solution.py:210
  54.2 21.9 %copy-start.3 = (bf16[1,512,128]{2,1,0:T(8,128)(2,1)S(1)}, bf16[1,512,128]{2,1,0:T(8,128)(2,1)}, u32[]{:S(2)}) copy-start(bf16[1,512,128]{2,1,0:T(8,128)(2,1)} %param.11) | copy-start | bytes 393220
  54.2 21.9 %copy-start.5 = (bf16[1,512,128]{2,1,0:T(8,128)(2,1)S(1)}, bf16[1,512,128]{2,1,0:T(8,128)(2,1)}, u32[]{:S(2)}) copy-start(bf16[1,512,128]{2,1,0:T(8,128)(2,1)} %param.12) | copy-start | bytes 393220
  54.2 21.9 %all-to-all-start.1 = ((bf16[64,16,128]{2,1,0:T(8,128)(2,1)}), bf16[64,16,128]{2,1,0:T(8,128)(2,1)S(1)}, u32[]{:S(2)}, u32[]{:S(2)}) async-start(bf16[64,16,128]{2,1,0:T(8,128)(2,1)} %conv.1), calls=%async_computation.1 | async-start | bytes 524288 | tf_op jit(solution)/shard_map/all_to_all | solution.py:223
  59.3 16.9 %copy-start.1 = (bf16[1,512,128]{2,1,0:T(8,128)(2,1)S(1)}, bf16[1,512,128]{2,1,0:T(8,128)(2,1)}, u32[]{:S(2)}) copy-start(bf16[1,512,128]{2,1,0:T(8,128)(2,1)} %param.10) | copy-start | bytes 393220
where the time goes:
time: 77.3 us; the launch traced here: 76.9 us
  blocking collectives  36 us (47%)
  waiting for transfers between devices  20.6 us (27%)
  starting transfers between devices  9.74 us (13%)
  Pallas kernels  6.25 us (8%)
  local copies, waits for them, and re-layouts  3.65 us (5%)
    all_to_all x1, blocking collectives, local(): here = lax.all_to_all(gated, 'ctx', 0, 0, tiled=True)  36 us
    all_to_all x1, waiting for transfers between devices, local(): back_here = lax.all_to_all(carried, 'ctx', 0, 0, tiled=True)  16.2 us
    pallas_call x6, Pallas kernels, call(): pl.pallas_call(kernel, out_shape=out, in_specs=[vmem] * len(args), out_sp...  6.25 us
    all_to_all x1, starting transfers between devices, local(): back_here = lax.all_to_all(carried, 'ctx', 0, 0, tiled=True)  5.05 us
    all_to_all x1, starting transfers between devices, local(): terms = lax.all_to_all(lag, 'dp', 0, 0, tiled=True)  4.69 us
    all_to_all x1, waiting for transfers between devices, local(): terms = lax.all_to_all(lag, 'dp', 0, 0, tiled=True)  4.39 us
    unnamed x24, local copies, waits for them, and re-layouts  3.65 us
  transfers between devices with their start and end apart: 2, of which 2 were waited for; matrix products, arithmetic and copies ran while one was open for 0% of the time, Pallas kernels for 4%

commit v1 on v0

--- a/solution.py
+++ b/solution.py
@@ -1,3 +1,4 @@
+import functools
 import math
 
 import jax
@@ -84,12 +85,28 @@
         out_ref[pl.ds(c, half, stride=chans), :] = signal[:, c * BLOCK : (c + 1) * BLOCK]
 
 
-def gate_kernel(key_ref, value_ref, grad_ref, query_ref, out_ref):
+def gate_kernel(key_hbm, value_hbm, grad_hbm, query_hbm, out_ref, held, sems):
     groups, both, _ = out_ref.shape
-    shape = (groups, both // 2, BLOCK)
-    kv = key_ref[...].astype(f32) * value_ref[...].astype(f32)
-    dz = grad_ref[...].astype(f32) * query_ref[...].astype(f32)
-    out_ref[...] = jnp.concatenate([kv.reshape(shape), dz.reshape(shape)], 1).astype(bf16)
+    pieces = sems.shape[1]
+    rows = key_hbm.shape[0] // pieces
+    part = groups // pieces
+
+    def copy(i, p):
+        span = pl.ds(p * rows, rows)
+        source = (key_hbm, value_hbm, grad_hbm, query_hbm)[i]
+        return pltpu.make_async_copy(source.at[span, :], held.at[i, span, :], sems.at[i, p])
+
+    for p in range(pieces):
+        for i in range(4):
+            copy(i, p).start()
+    for p in range(pieces):
+        for i in range(4):
+            copy(i, p).wait()
+        span = pl.ds(p * rows, rows)
+        key, value, grad, query = (held[i, span, :].astype(f32) for i in range(4))
+        shape = (part, both // 2, BLOCK)
+        kv, dz = (key * value).reshape(shape), (grad * query).reshape(shape)
+        out_ref[pl.ds(p * part, part)] = jnp.concatenate([kv, dz], 1).astype(bf16)
 
 
 def filter_kernel(filter_ref, forward_ref, turn_ref, middle_ref, spec_ref, rows):
@@ -100,20 +117,40 @@
     spec_ref[...] = forward_rows(rows, chans, half, False, forward_ref, turn_ref, middle_ref)
 
 
-def forward_kernel(
-    both_ref, forward_ref, back_ref, turn_ref, middle_ref, spec_ref, lag_ref, rows, out_rows
+def forward_kernel(both_ref, forward_ref, turn_ref, middle_ref, spec_ref, rows):
+    half, both, _ = both_ref.shape
+    rows[...] = both_ref[...].astype(f32).reshape(half * both, BLOCK)
+    spec_ref[...] = forward_rows(rows, both, half, True, forward_ref, turn_ref, middle_ref)
+
+
+def cross_kernel(
+    spec_ref, after_ref, back_ref, turn_ref, middle_ref, keep_ref, send_ref, out_rows
 ):
-    half, both, _ = both_ref.shape
-    chans = both // 2
-    rows[...] = both_ref[...].astype(f32).reshape(half * both, BLOCK)
-    spec = forward_rows(rows, both, half, True, forward_ref, turn_ref, middle_ref)
-    spec_ref[...] = spec
+    quads, own, chans, _ = keep_ref.shape
+    half = quads * 2 * own
     count = chans * half
-    kv_re, kv_im = spec[:count, :BLOCK], spec[:count, BLOCK:]
-    dz_re, dz_im = spec[count:, :BLOCK], spec[count:, BLOCK:]
+    kv_re, kv_im = spec_ref[:count, :BLOCK], spec_ref[:count, BLOCK:]
+    dz_re, dz_im = spec_ref[count:, :BLOCK], spec_ref[count:, BLOCK:]
     cross = jnp.concatenate([kv_re * dz_re + kv_im * dz_im, kv_im * dz_re - kv_re * dz_im], 1)
     inverse_rows(cross, chans, half, out_rows, back_ref, turn_ref, middle_ref)
-    lag_ref[...] = out_rows[...].reshape(half, chans, BLOCK).astype(bf16)
+    core = lax.rem(lax.axis_index("dp"), 2)
+    size = own * chans
+    for z in range(quads):
+        kept = pl.multiple_of((2 * z + core) * size, size)
+        sent = pl.multiple_of((2 * z + 1 - core) * size, size)
+        keep_ref[z] = out_rows[pl.ds(kept, size), :].reshape(own, chans, BLOCK)
+        send_ref[z] = out_rows[pl.ds(sent, size), :].reshape(own, chans, BLOCK).astype(bf16)
+
+
+def halve_kernel(keep_ref, other_ref, mine_ref, send_ref, *, step):
+    z = lax.div(lax.axis_index("dp"), 2)
+    bit = lax.rem(lax.div(z, step), 2)
+    count = mine_ref.shape[0]
+    mine, theirs = bit * count, (1 - bit) * count
+    mine_ref[...] = keep_ref[pl.ds(mine, count)] + other_ref[pl.ds(mine, count)].astype(f32)
+    send_ref[...] = (
+        keep_ref[pl.ds(theirs, count)] + other_ref[pl.ds(theirs, count)].astype(f32)
+    ).astype(bf16)
 
 
 def conv_kernel(spec_ref, filter_ref, back_ref, turn_ref, middle_ref, out_ref, out_rows):
@@ -141,12 +178,8 @@
     gv_ref[...] = (dkv * key_ref[...].astype(f32)).astype(bf16)
 
 
-def lag_kernel(terms_ref, out_ref, *, scale):
-    wide = terms_ref[...].astype(f32)
-    total = wide[0]
-    for g in range(1, wide.shape[0]):
-        total = total + wide[g]
-    total = total * scale
+def lag_kernel(keep_ref, other_ref, out_ref, *, scale):
+    total = (keep_ref[0] + other_ref[0].astype(f32)) * scale
     for a in range(total.shape[0]):
         out_ref[:, a * BLOCK : (a + 1) * BLOCK] = total[a]
 
@@ -182,7 +215,21 @@
     pieces = shape((half, both, BLOCK), bf16)
     work = 2 * chans * half * 256 * 768
 
-    gated = call(gate_kernel, pieces, key, value, grad, query, name="gate")
+    gated = pl.pallas_call(
+        gate_kernel,
+        out_shape=pieces,
+        in_specs=[pl.BlockSpec(memory_space=pltpu.HBM)] * 4,
+        out_specs=pl.BlockSpec(memory_space=pltpu.VMEM),
+        scratch_shapes=[
+            pltpu.VMEM((4, total, BLOCK), bf16),
+            pltpu.SemaphoreType.DMA((4, 4)),
+        ],
+        compiler_params=pltpu.CompilerParams(vmem_limit_bytes=63 * 2**20),
+        cost_estimate=pl.CostEstimate(
+            flops=total * BLOCK * 2, bytes_accessed=total * BLOCK * 12, transcendentals=0
+        ),
+        name="gate",
+    )(key, value, grad, query)
     here = lax.all_to_all(gated, "ctx", 0, 0, tiled=True)
     filter_spec = call(
         filter_kernel,
@@ -195,19 +242,17 @@
         flops=2 * work,
         name="filter",
     )
-    spec, lag = call(
+    spec = call(
         forward_kernel,
-        (shape((both * half, 2 * BLOCK), f32), shape((half, chans, BLOCK), bf16)),
+        shape((both * half, 2 * BLOCK), f32),
         here,
         forward,
-        back,
         turn,
         middle,
-        scratch=[(half * both, BLOCK), (half * chans, BLOCK)],
-        flops=4 * work,
+        scratch=[(half * both, BLOCK)],
+        flops=3 * work,
         name="forward",
     )
-    terms = lax.all_to_all(lag, "dp", 0, 0, tiled=True)
     carried = call(
         conv_kernel,
         pieces,
@@ -222,10 +267,37 @@
     )
     back_here = lax.all_to_all(carried, "ctx", 0, 0, tiled=True)
     own = half // groups
+    quads = groups // 2
+    quad = (own, chans, BLOCK)
+    keep, send = call(
+        cross_kernel,
+        (shape((quads, *quad), f32), shape((quads, *quad), bf16)),
+        spec,
+        carried,
+        back,
+        turn,
+        middle,
+        scratch=[(half * chans, BLOCK)],
+        flops=2 * work,
+        name="cross",
+    )
+    other = lax.ppermute(send, "dp", [(i, i ^ 1) for i in range(groups)])
+    step = quads // 2
+    while step:
+        keep, send = call(
+            functools.partial(halve_kernel, step=step),
+            (shape((step, *quad), f32), shape((step, *quad), bf16)),
+            keep,
+            other,
+            name="halve",
+        )
+        other = lax.ppermute(send, "dp", [(i, i ^ (2 * step)) for i in range(groups)])
+        step //= 2
     grad_filter = call(
         lambda *refs: lag_kernel(*refs, scale=1.0 / math.sqrt(seq * groups)),
         shape((chans, own * BLOCK), f32),
-        terms.reshape(groups, own, chans, BLOCK),
+        keep,
+        other,
         name="lag_sum",
     )
     grads = call(

time: 77.3 us -> 67.4 us (0.87)
  the two profiles are of different devices: /device:TPU:8 before, /device:TPU:6 now
where the time goes in v1:
time: 67.4 us; the launch traced here: 67 us
  starting transfers between devices  33 us (49%)
  waiting for transfers between devices  24.8 us (37%)
  Pallas kernels  8.39 us (12%)
  between operations  0.82 us (1%)
    all_to_all x1, starting transfers between devices, local(): here = lax.all_to_all(gated, 'ctx', 0, 0, tiled=True)  19.2 us
    all_to_all x1, waiting for transfers between devices, local(): here = lax.all_to_all(gated, 'ctx', 0, 0, tiled=True)  15.9 us
    ppermute x2, waiting for transfers between devices, local(): other = lax.ppermute(send, 'dp', [(i, i ^ 2 * step) for i in range(groups)])  7.62 us
    pallas_call x8, Pallas kernels, call(): pl.pallas_call(kernel, out_shape=out, in_specs=[vmem] * len(args), out_sp...  6.49 us
    ppermute x2, starting transfers between devices, local(): other = lax.ppermute(send, 'dp', [(i, i ^ 2 * step) for i in range(groups)])  6.45 us
    all_to_all x1, starting transfers between devices, local(): back_here = lax.all_to_all(carried, 'ctx', 0, 0, tiled=True)  5.45 us
    ppermute x1, starting transfers between devices, local(): other = lax.ppermute(send, 'dp', [(i, i ^ 1) for i in range(groups)])  1.92 us
    pallas_call x1, Pallas kernels, local(): pl.pallas_call(gate_kernel, out_shape=pieces, in_specs=[pl.BlockSpec(memo...  1.9 us
  transfers between devices with their start and end apart: 5, of which 4 were waited for; matrix products, arithmetic and copies ran while one was open for 0% of the time, Pallas kernels for 5%

profile of v1, /device:TPU:6, one launch (start us, length us, event | category | flops | bytes accessed | tf_op | source)
XLA Modules:
  0.0 67.0 jit_solution(4620317086586213988)
XLA Ops:
  0.6 0.0 copy-start.6
  0.6 1.9 %gate.1 = bf16[64,16,128]{2,1,0:T(8,128)(2,1)} custom-call(bf16[512,128]{1,0:T(8,128)(2,1)} %bitcast.7, bf16[512,128]{1,0:T(8,128)(2,1)} %bitcast.9, bf16[512,128]{1,0:T(8,128)(2,1)} %bitcast.11, bf16[512,128]{1,0:T(8,128)(2,1)} %bitcast.13), custom_call_target="tpu_custom_call" | custom-call | flops 131072 | bytes 786432 | tf_op jit(solution)/shard_map/gate/pallas_call | solution.py:218
  2.5 0.0 copy-start.3
  2.6 0.0 copy-start.4
  2.6 0.0 copy-start.7
  2.6 19.2 %all-to-all-start = ((bf16[64,16,128]{2,1,0:T(8,128)(2,1)}), bf16[64,16,128]{2,1,0:T(8,128)(2,1)S(1)}, u32[]{:S(2)}, u32[]{:S(2)}) async-start(bf16[64,16,128]{2,1,0:T(8,128)(2,1)} %gate.1), calls=%async_computation | async-start | bytes 524288 | tf_op jit(solution)/shard_map/all_to_all | solution.py:233
  21.8 0.0 copy-done.6
  21.8 0.0 copy-done.3
  21.8 0.0 copy-done.4
  21.8 0.0 copy-done.7
  21.8 0.6 filter.1.filter_ref
  22.4 0.0 copy-start.5
  22.4 15.9 %all-to-all-done.both_ref = bf16[64,16,128]{2,1,0:T(8,128)(2,1)S(1)} async-done(((bf16[64,16,128]{2,1,0:T(8,128)(2,1)}), bf16[64,16,128]{2,1,0:T(8,128)(2,1)S(1)}, u32[]{:S(2)}, u32[]{:S(2)}) %all-to-all-start) | async-done | bytes 262176 | tf_op jit(solution)/shard_map/all_to_all | solution.py:233
  38.3 0.9 %forward.1.spec_ref = f32[1024,256]{1,0:T(8,128)S(1)} custom-call(bf16[64,16,128]{2,1,0:T(8,128)(2,1)S(1)} %all-to-all-done.both_ref, bf16[128,192]{1,0:T(8,128)(2,1)S(1)} %copy-done.7, f32[2,64,128]{2,1,0:T(8,128)S(1)} %copy-done.4, bf16[768,256]{1,0:T(8,128)(2,1)S(1)} %copy-done.3), custom_call_target="tpu_custom_call" | custom-call | flops 603979776 | bytes 770048 | tf_op jit(solution)/shard_map/forward/pallas_call | solution.py:190
  39.2 0.0 copy-done.5
  39.2 1.8 %conv.1.after_ref = bf16[64,16,128]{2,1,0:T(8,128)(2,1)} custom-call(f32[1024,256]{1,0:T(8,128)S(1)} %forward.1.spec_ref, f32[512,256]{1,0:T(8,128)S(1)} %filter.1.filter_ref, bf16[64,384]{1,0:T(8,128)(2,1)S(1)} %copy-done.5, f32[2,64,128]{2,1,0:T(8,128)S(1)} %copy-done.4, bf16[768,256]{1,0:T(8,128)(2,1)S(1)} %copy-done.3), custom_call_target="tpu_custom_call" | custom-call | flops 805306368 | bytes 2080768 | tf_op jit(solution)/shard_map/conv/pallas_call | solution.py:190
  41.0 5.5 %all-to-all-start.1 = ((bf16[64,16,128]{2,1,0:T(8,128)(2,1)}), bf16[64,16,128]{2,1,0:T(8,128)(2,1)S(1)}, u32[]{:S(2)}, u32[]{:S(2)}) async-start(bf16[64,16,128]{2,1,0:T(8,128)(2,1)} %conv.1.after_ref), calls=%async_computation.1 | async-start | bytes 524288 | tf_op jit(solution)/shard_map/all_to_all | solution.py:268
  46.5 0.0 copy-start.2
  46.5 1.8 %cross.1 = (f32[4,8,8,128]{3,2,1,0:T(8,128)S(1)}, bf16[4,8,8,128]{3,2,1,0:T(8,128)(2,1)S(1)}) custom-call(f32[1024,256]{1,0:T(8,128)S(1)} %forward.1.spec_ref, bf16[64,16,128]{2,1,0:T(8,128)(2,1)} %conv.1.after_ref, bf16[64,384]{1,0:T(8,128)(2,1)S(1)} %copy-done.5, f32[2,64,128]{2,1,0:T(8,128)S(1)} %copy-done.4, bf16[768,256]{1,0:T(8,128)(2,1)S(1)} %copy-done.3), custom_call_target="tpu_custom_call" | custom-call | flops 402653184 | bytes 1818624 | tf_op jit(solution)/shard_map/cross/pallas_call | solution.py:190
  48.3 1.9 %collective-permute-start = (bf16[4,8,8,128]{3,2,1,0:T(8,128)(2,1)S(1)}, bf16[4,8,8,128]{3,2,1,0:T(8,128)(2,1)S(1)}, u32[]{:S(2)}, u32[]{:S(2)}) collective-permute-start(bf16[4,8,8,128]{3,2,1,0:T(8,128)(2,1)S(1)} %get-tuple-element.17), channel_id=1, source_target_pairs={{0,64},{64,0},{128,192},{192,128},{256,320},{320,256},{384,448},{4... | collective-permute-start | bytes 196616 | tf_op jit(solution)/shard_map/ppermute | solution.py:284
  50.3 1.2 %collective-permute-done.other_ref = bf16[4,8,8,128]{3,2,1,0:T(8,128)(2,1)S(1)} collective-permute-done((bf16[4,8,8,128]{3,2,1,0:T(8,128)(2,1)S(1)}, bf16[4,8,8,128]{3,2,1,0:T(8,128)(2,1)S(1)}, u32[]{:S(2)}, u32[]{:S(2)}) %collective-permute-start) | collective-permute-done | bytes 65568 | tf_op jit(solution)/shard_map/ppermute | solution.py:284
  51.5 0.0 copy-start.1
  51.5 0.0 copy-start
  51.5 4.4 %collective-permute-start.1 = (bf16[2,8,8,128]{3,2,1,0:T(8,128)(2,1)S(1)}, bf16[2,8,8,128]{3,2,1,0:T(8,128)(2,1)S(1)}, u32[]{:S(2)}, u32[]{:S(2)}) collective-permute-start(bf16[2,8,8,128]{3,2,1,0:T(8,128)(2,1)S(1)} %get-tuple-element.19), channel_id=1, source_target_pairs={{0,256},{64,320},{128,384},{192,448},{256,0},{320,64},{384,128},{4... | collective-permute-start | bytes 98312 | tf_op jit(solution)/shard_map/ppermute | solution.py:294
  55.9 4.0 %collective-permute-done.1.other_ref = bf16[2,8,8,128]{3,2,1,0:T(8,128)(2,1)S(1)} collective-permute-done((bf16[2,8,8,128]{3,2,1,0:T(8,128)(2,1)S(1)}, bf16[2,8,8,128]{3,2,1,0:T(8,128)(2,1)S(1)}, u32[]{:S(2)}, u32[]{:S(2)}) %collective-permute-start.1) | collective-permute-done | bytes 32800 | tf_op jit(solution)/shard_map/ppermute | solution.py:294
  60.0 2.0 %collective-permute-start.2 = (bf16[1,8,8,128]{3,2,1,0:T(8,128)(2,1)S(1)}, bf16[1,8,8,128]{3,2,1,0:T(8,128)(2,1)S(1)}, u32[]{:S(2)}, u32[]{:S(2)}) collective-permute-start(bf16[1,8,8,128]{3,2,1,0:T(8,128)(2,1)S(1)} %get-tuple-element.21), channel_id=1, source_target_pairs={{0,128},{64,192},{128,0},{192,64},{256,384},{320,448},{384,256},{4... | collective-permute-start | bytes 49160 | tf_op jit(solution)/shard_map/ppermute | solution.py:294
  62.0 3.6 %collective-permute-done.2.refs_1_ = bf16[1,8,8,128]{3,2,1,0:T(8,128)(2,1)S(1)} collective-permute-done((bf16[1,8,8,128]{3,2,1,0:T(8,128)(2,1)S(1)}, bf16[1,8,8,128]{3,2,1,0:T(8,128)(2,1)S(1)}, u32[]{:S(2)}, u32[]{:S(2)}) %collective-permute-start.2) | collective-permute-done | bytes 16416 | tf_op jit(solution)/shard_map/ppermute | solution.py:294
  65.6 0.6 lag_sum.1
  66.2 0.0 all-to-all-done.1.both_ref
  66.2 0.0 copy-done.2
  66.2 0.0 copy-done.1
  66.2 0.0 copy-done
  66.2 0.8 %final.1 = (bf16[512,128]{1,0:T(8,128)(2,1)}, bf16[512,128]{1,0:T(8,128)(2,1)}, bf16[512,128]{1,0:T(8,128)(2,1)}) custom-call(bf16[64,16,128]{2,1,0:T(8,128)(2,1)S(1)} %all-to-all-done.1.both_ref, bf16[512,128]{1,0:T(8,128)(2,1)S(1)} %bitcast.8, bf16[512,128]{1,0:T(8,128)(2,1)S(1)} %bitcast.10, bf16[512,128]{1,0:T(8,128)(2,1)S(1)} %bitcast.12), custom_call_target="tpu_custom_call" | custom-call | bytes 655360 | tf_op jit(solution)/shard_map/final/pallas_call | solution.py:190
  (2 shorter events, 0.0 us)
Async XLA Ops:
  0.6 21.1 %copy-start.6 = (f32[8,8192]{1,0:T(8,128)S(1)}, f32[8,8192]{1,0:T(8,128)}, u32[]{:S(2)}) copy-start(f32[8,8192]{1,0:T(8,128)} %filter_ref.1) | copy-start | bytes 786436
  2.5 19.2 %copy-start.3 = (bf16[768,256]{1,0:T(8,128)(2,1)S(1)}, bf16[768,256]{1,0:T(8,128)(2,1)}, u32[]{:S(2)}) copy-start(bf16[768,256]{1,0:T(8,128)(2,1)} %constant.10.clone.middle_ref) | copy-start | bytes 1179652
  2.6 19.2 %copy-start.4 = (f32[2,64,128]{2,1,0:T(8,128)S(1)}, f32[2,64,128]{2,1,0:T(8,128)}, u32[]{:S(2)}) copy-start(f32[2,64,128]{2,1,0:T(8,128)} %constant.11.clone.turn_ref) | copy-start | bytes 196612
  2.6 19.2 %copy-start.7 = (bf16[128,192]{1,0:T(8,128)(2,1)S(1)}, bf16[128,192]{1,0:T(8,128)(2,1)}, u32[]{:S(2)}) copy-start(bf16[128,192]{1,0:T(8,128)(2,1)} %constant.8.clone.forward_ref) | copy-start | bytes 147460
  2.6 35.7 %all-to-all-start = ((bf16[64,16,128]{2,1,0:T(8,128)(2,1)}), bf16[64,16,128]{2,1,0:T(8,128)(2,1)S(1)}, u32[]{:S(2)}, u32[]{:S(2)}) async-start(bf16[64,16,128]{2,1,0:T(8,128)(2,1)} %gate.1), calls=%async_computation | async-start | bytes 524288 | tf_op jit(solution)/shard_map/all_to_all | solution.py:233
  22.4 16.8 %copy-start.5 = (bf16[64,384]{1,0:T(8,128)(2,1)S(1)}, bf16[64,384]{1,0:T(8,128)(2,1)}, u32[]{:S(2)}) copy-start(bf16[64,384]{1,0:T(8,128)(2,1)} %constant.9.clone.back_ref) | copy-start | bytes 147460
  41.0 25.2 %all-to-all-start.1 = ((bf16[64,16,128]{2,1,0:T(8,128)(2,1)}), bf16[64,16,128]{2,1,0:T(8,128)(2,1)S(1)}, u32[]{:S(2)}, u32[]{:S(2)}) async-start(bf16[64,16,128]{2,1,0:T(8,128)(2,1)} %conv.1.after_ref), calls=%async_computation.1 | async-start | bytes 524288 | tf_op jit(solution)/shard_map/all_to_all | solution.py:268
  46.5 19.7 %copy-start.2 = (bf16[1,512,128]{2,1,0:T(8,128)(2,1)S(1)}, bf16[1,512,128]{2,1,0:T(8,128)(2,1)}, u32[]{:S(2)}) copy-start(bf16[1,512,128]{2,1,0:T(8,128)(2,1)} %param.12) | copy-start | bytes 393220
  48.3 3.1 %collective-permute-start = (bf16[4,8,8,128]{3,2,1,0:T(8,128)(2,1)S(1)}, bf16[4,8,8,128]{3,2,1,0:T(8,128)(2,1)S(1)}, u32[]{:S(2)}, u32[]{:S(2)}) collective-permute-start(bf16[4,8,8,128]{3,2,1,0:T(8,128)(2,1)S(1)} %get-tuple-element.17), channel_id=1, source_target_pairs={{0,64},{64,0},{128,192},{192,128},{256,320},{320,256},{384,448},{4... | collective-permute-start | bytes 196616 | tf_op jit(solution)/shard_map/ppermute | solution.py:284
  51.5 14.8 %copy-start.1 = (bf16[1,512,128]{2,1,0:T(8,128)(2,1)S(1)}, bf16[1,512,128]{2,1,0:T(8,128)(2,1)}, u32[]{:S(2)}) copy-start(bf16[1,512,128]{2,1,0:T(8,128)(2,1)} %param.11) | copy-start | bytes 393220
  51.5 14.7 %copy-start = (bf16[1,512,128]{2,1,0:T(8,128)(2,1)S(1)}, bf16[1,512,128]{2,1,0:T(8,128)(2,1)}, u32[]{:S(2)}) copy-start(bf16[1,512,128]{2,1,0:T(8,128)(2,1)} %param.10) | copy-start | bytes 393220
  51.5 8.4 %collective-permute-start.1 = (bf16[2,8,8,128]{3,2,1,0:T(8,128)(2,1)S(1)}, bf16[2,8,8,128]{3,2,1,0:T(8,128)(2,1)S(1)}, u32[]{:S(2)}, u32[]{:S(2)}) collective-permute-start(bf16[2,8,8,128]{3,2,1,0:T(8,128)(2,1)S(1)} %get-tuple-element.19), channel_id=1, source_target_pairs={{0,256},{64,320},{128,384},{192,448},{256,0},{320,64},{384,128},{4... | collective-permute-start | bytes 98312 | tf_op jit(solution)/shard_map/ppermute | solution.py:294
  60.0 5.6 %collective-permute-start.2 = (bf16[1,8,8,128]{3,2,1,0:T(8,128)(2,1)S(1)}, bf16[1,8,8,128]{3,2,1,0:T(8,128)(2,1)S(1)}, u32[]{:S(2)}, u32[]{:S(2)}) collective-permute-start(bf16[1,8,8,128]{3,2,1,0:T(8,128)(2,1)S(1)} %get-tuple-element.21), channel_id=1, source_target_pairs={{0,128},{64,192},{128,0},{192,64},{256,384},{320,448},{384,256},{4... | collective-permute-start | bytes 49160 | tf_op jit(solution)/shard_map/ppermute | solution.py:294

commit v2 on v1

--- a/solution.py
+++ b/solution.py
@@ -14,6 +14,23 @@
 f32 = jnp.float32
 
 
+FAR_IN, FAR_OUT = 58, 58
+HINT = 30 * 10**9
+
+
+def slots(count, far):
+    return [m ^ far for m in range(count)]
+
+
+def swap_slots(blocks, far):
+    rest = blocks.shape[1:]
+    for bit in (1 << b for b in range(6)):
+        if far & bit and bit < blocks.shape[0]:
+            pairs = blocks.reshape(blocks.shape[0] // (2 * bit), 2, bit, *rest)
+            blocks = jnp.concatenate([pairs[:, 1:], pairs[:, :1]], 1).reshape(-1, *rest)
+    return blocks
+
+
 def split_table(table):
     high = table.astype(bf16)
     return high, (table - high.astype(np.float64)).astype(bf16)
@@ -25,15 +42,18 @@
     first = 2.0 * math.pi * np.outer(k, np.arange(half)) / (2 * half)
     turn = 2.0 * math.pi * np.outer(k, np.arange(BLOCK)) / length
     block = 2.0 * math.pi * np.outer(np.arange(BLOCK), np.arange(BLOCK)) / BLOCK
-    first_high, first_low = split_table(np.concatenate([np.cos(first), -np.sin(first)], 0))
+    came = slots(half, FAR_IN)
+    first_high, first_low = split_table(np.concatenate([np.cos(first), -np.sin(first)], 0)[:, came])
     last_high, last_low = split_table(
         np.concatenate([np.cos(first).T, -np.sin(first).T], 1) * (2.0 / length)
     )
+    back = np.concatenate([last_high, last_high, last_low], 1)
     cos, sin = np.cos(block), np.sin(block)
     mid_high, mid_low = split_table(np.block([[cos, -sin], [sin, cos]]))
     return {
         "forward": np.concatenate([first_high, first_high, first_low], 1),
-        "back": np.concatenate([last_high, last_high, last_low], 1),
+        "back": back[slots(half, FAR_OUT)],
+        "lag": back,
         "middle": np.concatenate([mid_high, mid_high, mid_low], 0),
         "turn": np.stack([np.cos(turn), np.sin(turn)]).astype(np.float32),
     }
@@ -106,14 +126,15 @@
         key, value, grad, query = (held[i, span, :].astype(f32) for i in range(4))
         shape = (part, both // 2, BLOCK)
         kv, dz = (key * value).reshape(shape), (grad * query).reshape(shape)
-        out_ref[pl.ds(p * part, part)] = jnp.concatenate([kv, dz], 1).astype(bf16)
+        to = (p * part ^ FAR_IN) // part * part
+        out_ref[pl.ds(to, part)] = swap_slots(jnp.concatenate([kv, dz], 1).astype(bf16), FAR_IN)
 
 
 def filter_kernel(filter_ref, forward_ref, turn_ref, middle_ref, spec_ref, rows):
     chans, seq = filter_ref.shape
     half = seq // BLOCK
-    for a in range(half):
-        rows[pl.ds(a * chans, chans), :] = filter_ref[:, a * BLOCK : (a + 1) * BLOCK]
+    for a, slot in enumerate(slots(half, FAR_IN)):
+        rows[pl.ds(slot * chans, chans), :] = filter_ref[:, a * BLOCK : (a + 1) * BLOCK]
     spec_ref[...] = forward_rows(rows, chans, half, False, forward_ref, turn_ref, middle_ref)
 
 
@@ -123,37 +144,29 @@
     spec_ref[...] = forward_rows(rows, both, half, True, forward_ref, turn_ref, middle_ref)
 
 
-def cross_kernel(
-    spec_ref, after_ref, back_ref, turn_ref, middle_ref, keep_ref, send_ref, out_rows
-):
-    quads, own, chans, _ = keep_ref.shape
-    half = quads * 2 * own
+def cross_kernel(spec_ref, back_ref, turn_ref, middle_ref, keep_ref, send_ref, out_rows):
+    pairs, cores, own, chans, _ = keep_ref.shape
+    half = 2 * pairs * cores * own
     count = chans * half
     kv_re, kv_im = spec_ref[:count, :BLOCK], spec_ref[:count, BLOCK:]
     dz_re, dz_im = spec_ref[count:, :BLOCK], spec_ref[count:, BLOCK:]
     cross = jnp.concatenate([kv_re * dz_re + kv_im * dz_im, kv_im * dz_re - kv_re * dz_im], 1)
     inverse_rows(cross, chans, half, out_rows, back_ref, turn_ref, middle_ref)
-    core = lax.rem(lax.axis_index("dp"), 2)
-    size = own * chans
-    for z in range(quads):
-        kept = pl.multiple_of((2 * z + core) * size, size)
-        sent = pl.multiple_of((2 * z + 1 - core) * size, size)
-        keep_ref[z] = out_rows[pl.ds(kept, size), :].reshape(own, chans, BLOCK)
-        send_ref[z] = out_rows[pl.ds(sent, size), :].reshape(own, chans, BLOCK).astype(bf16)
-
-
-def halve_kernel(keep_ref, other_ref, mine_ref, send_ref, *, step):
-    z = lax.div(lax.axis_index("dp"), 2)
-    bit = lax.rem(lax.div(z, step), 2)
-    count = mine_ref.shape[0]
-    mine, theirs = bit * count, (1 - bit) * count
-    mine_ref[...] = keep_ref[pl.ds(mine, count)] + other_ref[pl.ds(mine, count)].astype(f32)
-    send_ref[...] = (
-        keep_ref[pl.ds(theirs, count)] + other_ref[pl.ds(theirs, count)].astype(f32)
-    ).astype(bf16)
-
-
-def conv_kernel(spec_ref, filter_ref, back_ref, turn_ref, middle_ref, out_ref, out_rows):
+    bit = lax.div(lax.axis_index("dp"), 4)
+    size = out_rows.shape[0] // 2
+    kept = pl.multiple_of(bit * size, size)
+    sent = pl.multiple_of((1 - bit) * size, size)
+    keep_ref[...] = out_rows[pl.ds(kept, size), :].reshape(keep_ref.shape)
+    send_ref[...] = out_rows[pl.ds(sent, size), :].reshape(send_ref.shape).astype(bf16)
+
+
+def halve_kernel(keep_ref, other_ref, mine_ref, send_ref, *, axis_bit):
+    bit = lax.rem(lax.div(lax.axis_index("dp"), axis_bit), 2)
+    mine_ref[...] = keep_ref[bit] + other_ref[bit].astype(f32)
+    send_ref[...] = (keep_ref[1 - bit] + other_ref[1 - bit].astype(f32)).astype(bf16)
+
+
+def conv_kernel(spec_ref, filter_ref, back_ref, turn_ref, middle_ref, after_ref, out_ref, out_rows):
     half, both, _ = out_ref.shape
     count = half * both // 2
     f_re, f_im = filter_ref[:, :BLOCK], filter_ref[:, BLOCK:]
@@ -167,10 +180,27 @@
     out_ref[...] = out_rows[...].reshape(half, both, BLOCK).astype(bf16)
 
 
-def final_kernel(both_ref, key_ref, value_ref, grad_ref, gq_ref, gk_ref, gv_ref):
+def final_kernel(
+    both_ref,
+    key_ref,
+    value_ref,
+    grad_ref,
+    keep_ref,
+    other_ref,
+    gq_ref,
+    gk_ref,
+    gv_ref,
+    gf_ref,
+    *,
+    scale,
+):
+    core = lax.rem(lax.axis_index("dp"), 2)
+    lags = (keep_ref[...] + other_ref[1 - core].astype(f32)) * scale
+    for a in range(lags.shape[0]):
+        gf_ref[:, a * BLOCK : (a + 1) * BLOCK] = lags[a]
     groups, both, _ = both_ref.shape
     chans = both // 2
-    wide = both_ref[...].astype(f32)
+    wide = swap_slots(both_ref[...], FAR_OUT).astype(f32)
     conv = wide[:, :chans, :].reshape(groups * chans, BLOCK)
     dkv = wide[:, chans:, :].reshape(groups * chans, BLOCK)
     gq_ref[...] = (grad_ref[...].astype(f32) * conv).astype(bf16)
@@ -178,19 +208,14 @@
     gv_ref[...] = (dkv * key_ref[...].astype(f32)).astype(bf16)
 
 
-def lag_kernel(keep_ref, other_ref, out_ref, *, scale):
-    total = (keep_ref[0] + other_ref[0].astype(f32)) * scale
-    for a in range(total.shape[0]):
-        out_ref[:, a * BLOCK : (a + 1) * BLOCK] = total[a]
-
-
-def call(kernel, out, *args, scratch=(), flops=0, name=None):
+def call(kernel, out, *args, scratch=(), flops=0, any_space=0, name=None):
     nbytes = sum(math.prod(a.shape) * a.dtype.itemsize for a in args)
     vmem = pl.BlockSpec(memory_space=pltpu.VMEM)
     return pl.pallas_call(
         kernel,
         out_shape=out,
-        in_specs=[vmem] * len(args),
+        in_specs=[vmem] * (len(args) - any_space)
+        + [pl.BlockSpec(memory_space=pl.ANY)] * any_space,
         out_specs=jax.tree.map(lambda _: vmem, out),
         scratch_shapes=[pltpu.VMEM(shape, f32) for shape in scratch],
         compiler_params=pltpu.CompilerParams(vmem_limit_bytes=40 * 2**20),
@@ -207,7 +232,7 @@
     both = 2 * chans
     tables = {name: jnp.asarray(table) for name, table in make_tables(half, seq).items()}
     forward, back = tables["forward"], tables["back"]
-    turn, middle = tables["turn"], tables["middle"]
+    turn, middle, lag_back = tables["turn"], tables["middle"], tables["lag"]
     query, key, value, grad = (
         x.reshape(total, BLOCK) for x in (query_gate, key_gate, value_gate, grad_out)
     )
@@ -230,7 +255,9 @@
         ),
         name="gate",
     )(key, value, grad, query)
-    here = lax.all_to_all(gated, "ctx", 0, 0, tiled=True)
+    here = lax.all_to_all(
+        gated, "ctx", 0, 0, tiled=True, axis_index_groups=[slots(half, FAR_IN)]
+    )
     filter_spec = call(
         filter_kernel,
         shape((chans * half, 2 * BLOCK), f32),
@@ -253,6 +280,21 @@
         flops=3 * work,
         name="forward",
     )
+    own = half // groups
+    quads = groups // 2
+    quad = (own, chans, BLOCK)
+    keep, send = call(
+        cross_kernel,
+        (shape((2, 2, *quad), f32), shape((2, 2, *quad), bf16)),
+        spec,
+        lag_back,
+        turn,
+        middle,
+        scratch=[(half * chans, BLOCK)],
+        flops=2 * work,
+        name="cross",
+    )
+    other = lax.ppermute(send, "dp", [(i, i ^ 4) for i in range(groups)])
     carried = call(
         conv_kernel,
         pieces,
@@ -261,52 +303,42 @@
         back,
         turn,
         middle,
+        send,
         scratch=[(half * both, BLOCK)],
         flops=4 * work,
+        any_space=1,
         name="conv",
     )
-    back_here = lax.all_to_all(carried, "ctx", 0, 0, tiled=True)
-    own = half // groups
-    quads = groups // 2
-    quad = (own, chans, BLOCK)
     keep, send = call(
-        cross_kernel,
-        (shape((quads, *quad), f32), shape((quads, *quad), bf16)),
-        spec,
-        carried,
-        back,
-        turn,
-        middle,
-        scratch=[(half * chans, BLOCK)],
-        flops=2 * work,
-        name="cross",
-    )
-    other = lax.ppermute(send, "dp", [(i, i ^ 1) for i in range(groups)])
-    step = quads // 2
-    while step:
-        keep, send = call(
-            functools.partial(halve_kernel, step=step),
-            (shape((step, *quad), f32), shape((step, *quad), bf16)),
-            keep,
-            other,
-            name="halve",
-        )
-        other = lax.ppermute(send, "dp", [(i, i ^ (2 * step)) for i in range(groups)])
-        step //= 2
-    grad_filter = call(
-        lambda *refs: lag_kernel(*refs, scale=1.0 / math.sqrt(seq * groups)),
-        shape((chans, own * BLOCK), f32),
+        functools.partial(halve_kernel, axis_bit=2),
+        (shape((2, *quad), f32), shape((2, *quad), bf16)),
         keep,
         other,
-        name="lag_sum",
-    )
-    grads = call(
-        final_kernel,
-        (shape((total, BLOCK), bf16),) * 3,
+        flops=HINT,
+        name="halve",
+    )
+    other = lax.ppermute(send, "dp", [(i, i ^ 2) for i in range(groups)])
+    keep, send = call(
+        functools.partial(halve_kernel, axis_bit=1),
+        (shape(quad, f32), shape(quad, bf16)),
+        keep,
+        other,
+        name="pair",
+    )
+    cores = [[2 * z, 2 * z + 1] for z in range(quads)]
+    other = lax.all_gather(send, "dp", axis=0, axis_index_groups=cores)
+    back_here = lax.all_to_all(
+        carried, "ctx", 0, 0, tiled=True, axis_index_groups=[slots(half, FAR_OUT)]
+    )
+    *grads, grad_filter = call(
+        functools.partial(final_kernel, scale=1.0 / math.sqrt(seq * groups)),
+        (shape((total, BLOCK), bf16),) * 3 + (shape((chans, own * BLOCK), f32),),
         back_here,
         key,
         value,
         grad,
+        keep,
+        other,
         name="final",
     )
     return tuple(g[None] for g in grads) + (grad_filter,)

time: 67.4 us -> 64.1 us (0.951)
  the two profiles are of different devices: /device:TPU:6 before, /device:TPU:1 now
where the time goes in v2:
time: 64.1 us; the launch traced here: 63.7 us
  starting transfers between devices  42.3 us (66%)
  waiting for transfers between devices  11.7 us (18%)
  Pallas kernels  6.8 us (11%)
  blocking collectives  2.06 us (3%)
  between operations  0.84 us (1%)
    all_to_all x1, starting transfers between devices, local(): lax.all_to_all(gated, 'ctx', 0, 0, tiled=True, axis_index_groups=[slots(h...  20.4 us
    all_to_all x1, starting transfers between devices, local(): lax.all_to_all(carried, 'ctx', 0, 0, tiled=True, axis_index_groups=[slots...  14.9 us
    ppermute x1, waiting for transfers between devices, local(): other = lax.ppermute(send, 'dp', [(i, i ^ 2) for i in range(groups)])  5.96 us
    all_to_all x1, waiting for transfers between devices, local(): lax.all_to_all(gated, 'ctx', 0, 0, tiled=True, axis_index_groups=[slots(h...  5.76 us
    pallas_call x7, Pallas kernels, call(): pl.pallas_call(kernel, out_shape=out, in_specs=[vmem] * (len(args) - any_...  4.9 us
    ppermute x1, starting transfers between devices, local(): other = lax.ppermute(send, 'dp', [(i, i ^ 4) for i in range(groups)])  4.01 us
    ppermute x1, starting transfers between devices, local(): other = lax.ppermute(send, 'dp', [(i, i ^ 2) for i in range(groups)])  2.89 us
    all_gather x1, blocking collectives, local(): other = lax.all_gather(send, 'dp', axis=0, axis_index_groups=cores)  2.06 us
  transfers between devices with their start and end apart: 4, of which 2 were waited for; matrix products, arithmetic and copies ran while one was open for 0% of the time, Pallas kernels for 4%

profile of v2, /device:TPU:1, one launch (start us, length us, event | category | flops | bytes accessed | tf_op | source)
XLA Modules:
  0.0 63.7 jit_solution(4940738823548046513)
XLA Ops:
  0.6 0.0 copy-start.6
  0.6 1.9 %gate.1 = bf16[64,16,128]{2,1,0:T(8,128)(2,1)} custom-call(bf16[512,128]{1,0:T(8,128)(2,1)} %bitcast.8, bf16[512,128]{1,0:T(8,128)(2,1)} %bitcast.10, bf16[512,128]{1,0:T(8,128)(2,1)} %bitcast.12, bf16[512,128]{1,0:T(8,128)(2,1)} %bitcast.15), custom_call_target="tpu_custom_call" | custom-call | flops 131072 | bytes 786432 | tf_op jit(solution)/shard_map/gate/pallas_call | solution.py:243
  2.5 0.0 copy-start.3
  2.6 0.0 copy-start.4
  2.6 0.0 copy-start.7
  2.6 20.4 %all-to-all-start = ((bf16[64,16,128]{2,1,0:T(8,128)(2,1)}), bf16[64,16,128]{2,1,0:T(8,128)(2,1)S(1)}, u32[]{:S(2)}, u32[]{:S(2)}) async-start(bf16[64,16,128]{2,1,0:T(8,128)(2,1)} %gate.1), calls=%async_computation | async-start | bytes 524288 | tf_op jit(solution)/shard_map/all_to_all | solution.py:258
  23.0 0.0 copy-done.6
  23.1 0.0 copy-done.3
  23.1 0.0 copy-done.4
  23.1 0.0 copy-done.7
  23.1 0.6 filter.1.filter_ref
  23.6 0.0 copy-start.5
  23.7 5.8 %all-to-all-done.both_ref = bf16[64,16,128]{2,1,0:T(8,128)(2,1)S(1)} async-done(((bf16[64,16,128]{2,1,0:T(8,128)(2,1)}), bf16[64,16,128]{2,1,0:T(8,128)(2,1)S(1)}, u32[]{:S(2)}, u32[]{:S(2)}) %all-to-all-start) | async-done | bytes 262176 | tf_op jit(solution)/shard_map/all_to_all | solution.py:258
  29.4 0.9 %forward.1.spec_ref = f32[1024,256]{1,0:T(8,128)S(1)} custom-call(bf16[64,16,128]{2,1,0:T(8,128)(2,1)S(1)} %all-to-all-done.both_ref, bf16[128,192]{1,0:T(8,128)(2,1)S(1)} %copy-done.7, f32[2,64,128]{2,1,0:T(8,128)S(1)} %copy-done.4, bf16[768,256]{1,0:T(8,128)(2,1)S(1)} %copy-done.3), custom_call_target="tpu_custom_call" | custom-call | flops 603979776 | bytes 770048 | tf_op jit(solution)/shard_map/forward/pallas_call | solution.py:214
  30.3 0.0 copy-done.5
  30.3 0.0 copy-start.8
  30.3 0.8 %cross.1 = (f32[2,2,8,8,128]{4,3,2,1,0:T(8,128)S(1)}, bf16[2,2,8,8,128]{4,3,2,1,0:T(8,128)(2,1)S(1)}) custom-call(f32[1024,256]{1,0:T(8,128)S(1)} %forward.1.spec_ref, bf16[64,384]{1,0:T(8,128)(2,1)S(1)} %copy-done.5, f32[2,64,128]{2,1,0:T(8,128)S(1)} %copy-done.4, bf16[768,256]{1,0:T(8,128)(2,1)S(1)} %copy-done.3), custom_call_target="tpu_custom_call" | custom-call | flops 402653184 | bytes 1556480 | tf_op jit(solution)/shard_map/cross/pallas_call | solution.py:214
  31.1 4.0 %collective-permute-start = (bf16[2,2,8,8,128]{4,3,2,1,0:T(8,128)(2,1)S(1)}, bf16[2,2,8,8,128]{4,3,2,1,0:T(8,128)(2,1)S(1)}, u32[]{:S(2)}, u32[]{:S(2)}) collective-permute-start(bf16[2,2,8,8,128]{4,3,2,1,0:T(8,128)(2,1)S(1)} %get-tuple-element.14.after_ref), channel_id=1, source_target_pairs={{0,256},{64,320},{128,384},{192,448},{256,0},{320,64},{384,128},{4... | collective-permute-start | bytes 196616 | tf_op jit(solution)/shard_map/ppermute | solution.py:297
  35.1 0.0 copy-done.8
  35.2 1.8 %conv.1 = bf16[64,16,128]{2,1,0:T(8,128)(2,1)} custom-call(f32[1024,256]{1,0:T(8,128)S(1)} %forward.1.spec_ref, f32[512,256]{1,0:T(8,128)S(1)} %filter.1.filter_ref, bf16[64,384]{1,0:T(8,128)(2,1)S(1)} %copy-done.8, f32[2,64,128]{2,1,0:T(8,128)S(1)} %copy-done.4, bf16[768,256]{1,0:T(8,128)(2,1)S(1)} %copy-done.3, ...), custom_call_target="tpu_custom_call" | custom-call | flops 805306368 | bytes 2146304 | tf_op jit(solution)/shard_map/conv/pallas_call | solution.py:214
  37.0 14.9 %all-to-all-start.1 = ((bf16[64,16,128]{2,1,0:T(8,128)(2,1)}), bf16[64,16,128]{2,1,0:T(8,128)(2,1)S(1)}, u32[]{:S(2)}, u32[]{:S(2)}) async-start(bf16[64,16,128]{2,1,0:T(8,128)(2,1)} %conv.1), calls=%async_computation.1 | async-start | bytes 524288 | tf_op jit(solution)/shard_map/all_to_all | solution.py:330
  51.9 0.0 collective-permute-done.other_ref
  51.9 0.0 copy-start.1
  51.9 0.0 copy-start.2
  52.0 0.0 copy-start
  52.0 2.9 %collective-permute-start.1 = (bf16[2,8,8,128]{3,2,1,0:T(8,128)(2,1)S(1)}, bf16[2,8,8,128]{3,2,1,0:T(8,128)(2,1)S(1)}, u32[]{:S(2)}, u32[]{:S(2)}) collective-permute-start(bf16[2,8,8,128]{3,2,1,0:T(8,128)(2,1)S(1)} %get-tuple-element.17), channel_id=1, source_target_pairs={{0,128},{64,192},{128,0},{192,64},{256,384},{320,448},{384,256},{4... | collective-permute-start | bytes 98312 | tf_op jit(solution)/shard_map/ppermute | solution.py:320
  54.9 6.0 %collective-permute-done.1.other_ref = bf16[2,8,8,128]{3,2,1,0:T(8,128)(2,1)S(1)} collective-permute-done((bf16[2,8,8,128]{3,2,1,0:T(8,128)(2,1)S(1)}, bf16[2,8,8,128]{3,2,1,0:T(8,128)(2,1)S(1)}, u32[]{:S(2)}, u32[]{:S(2)}) %collective-permute-start.1) | collective-permute-done | bytes 32800 | tf_op jit(solution)/shard_map/ppermute | solution.py:320
  60.9 2.1 %all-gather = bf16[16,8,128]{2,1,0:T(8,128)(2,1)S(1)} all-gather(bf16[8,8,128]{2,1,0:T(8,128)(2,1)S(1)} %get-tuple-element.19), channel_id=2, replica_groups={{0,64},{128,192},{256,320},{384,448},{1,65},{129,193},{257,321},{385,44..., dimensions={0}, use_global_device_ids=true | all-gather | bytes 49152 | tf_op jit(solution)/shard_map/all_gather | solution.py:329
  62.9 0.0 all-to-all-done.1.both_ref
  62.9 0.0 copy-done.1
  62.9 0.0 copy-done.2
  62.9 0.0 copy-done
  63.0 0.8 %final.1 = (bf16[512,128]{1,0:T(8,128)(2,1)}, bf16[512,128]{1,0:T(8,128)(2,1)}, bf16[512,128]{1,0:T(8,128)(2,1)}, f32[8,1024]{1,0:T(8,128)}) custom-call(bf16[64,16,128]{2,1,0:T(8,128)(2,1)S(1)} %all-to-all-done.1.both_ref, bf16[512,128]{1,0:T(8,128)(2,1)S(1)} %bitcast.9, bf16[512,128]{1,0:T(8,128)(2,1)S(1)} %bitcast.11, bf16[512,128]{1,0:T(8,128)(2,1)S(1)} %bitcast.13, ...), custom_call_target="tpu_custom_call" | custom-call | bytes 720896 | tf_op jit(solution)/shard_map/final/pallas_call | solution.py:214
  (2 shorter events, 0.0 us)
Async XLA Ops:
  0.6 22.4 %copy-start.6 = (f32[8,8192]{1,0:T(8,128)S(1)}, f32[8,8192]{1,0:T(8,128)}, u32[]{:S(2)}) copy-start(f32[8,8192]{1,0:T(8,128)} %filter_ref.1) | copy-start | bytes 786436
  2.5 20.5 %copy-start.3 = (bf16[768,256]{1,0:T(8,128)(2,1)S(1)}, bf16[768,256]{1,0:T(8,128)(2,1)}, u32[]{:S(2)}) copy-start(bf16[768,256]{1,0:T(8,128)(2,1)} %constant.13.clone.middle_ref) | copy-start | bytes 1179652
  2.6 20.5 %copy-start.4 = (f32[2,64,128]{2,1,0:T(8,128)S(1)}, f32[2,64,128]{2,1,0:T(8,128)}, u32[]{:S(2)}) copy-start(f32[2,64,128]{2,1,0:T(8,128)} %constant.14.clone.turn_ref) | copy-start | bytes 196612
  2.6 20.5 %copy-start.7 = (bf16[128,192]{1,0:T(8,128)(2,1)S(1)}, bf16[128,192]{1,0:T(8,128)(2,1)}, u32[]{:S(2)}) copy-start(bf16[128,192]{1,0:T(8,128)(2,1)} %constant.10.clone.forward_ref) | copy-start | bytes 147460
  2.6 26.8 %all-to-all-start = ((bf16[64,16,128]{2,1,0:T(8,128)(2,1)}), bf16[64,16,128]{2,1,0:T(8,128)(2,1)S(1)}, u32[]{:S(2)}, u32[]{:S(2)}) async-start(bf16[64,16,128]{2,1,0:T(8,128)(2,1)} %gate.1), calls=%async_computation | async-start | bytes 524288 | tf_op jit(solution)/shard_map/all_to_all | solution.py:258
  23.6 6.6 %copy-start.5 = (bf16[64,384]{1,0:T(8,128)(2,1)S(1)}, bf16[64,384]{1,0:T(8,128)(2,1)}, u32[]{:S(2)}) copy-start(bf16[64,384]{1,0:T(8,128)(2,1)} %constant.12.clone.back_ref) | copy-start | bytes 147460
  30.3 4.8 %copy-start.8 = (bf16[64,384]{1,0:T(8,128)(2,1)S(1)}, bf16[64,384]{1,0:T(8,128)(2,1)}, u32[]{:S(2)}) copy-start(bf16[64,384]{1,0:T(8,128)(2,1)} %constant.11.clone.back_ref) | copy-start | bytes 147460
  31.1 20.8 %collective-permute-start = (bf16[2,2,8,8,128]{4,3,2,1,0:T(8,128)(2,1)S(1)}, bf16[2,2,8,8,128]{4,3,2,1,0:T(8,128)(2,1)S(1)}, u32[]{:S(2)}, u32[]{:S(2)}) collective-permute-start(bf16[2,2,8,8,128]{4,3,2,1,0:T(8,128)(2,1)S(1)} %get-tuple-element.14.after_ref), channel_id=1, source_target_pairs={{0,256},{64,320},{128,384},{192,448},{256,0},{320,64},{384,128},{4... | collective-permute-start | bytes 196616 | tf_op jit(solution)/shard_map/ppermute | solution.py:297
  37.0 25.9 %all-to-all-start.1 = ((bf16[64,16,128]{2,1,0:T(8,128)(2,1)}), bf16[64,16,128]{2,1,0:T(8,128)(2,1)S(1)}, u32[]{:S(2)}, u32[]{:S(2)}) async-start(bf16[64,16,128]{2,1,0:T(8,128)(2,1)} %conv.1), calls=%async_computation.1 | async-start | bytes 524288 | tf_op jit(solution)/shard_map/all_to_all | solution.py:330
  51.9 11.0 %copy-start.1 = (bf16[1,512,128]{2,1,0:T(8,128)(2,1)S(1)}, bf16[1,512,128]{2,1,0:T(8,128)(2,1)}, u32[]{:S(2)}) copy-start(bf16[1,512,128]{2,1,0:T(8,128)(2,1)} %param.12) | copy-start | bytes 393220
  51.9 11.0 %copy-start.2 = (bf16[1,512,128]{2,1,0:T(8,128)(2,1)S(1)}, bf16[1,512,128]{2,1,0:T(8,128)(2,1)}, u32[]{:S(2)}) copy-start(bf16[1,512,128]{2,1,0:T(8,128)(2,1)} %param.13) | copy-start | bytes 393220
  52.0 11.0 %copy-start = (bf16[1,512,128]{2,1,0:T(8,128)(2,1)S(1)}, bf16[1,512,128]{2,1,0:T(8,128)(2,1)}, u32[]{:S(2)}) copy-start(bf16[1,512,128]{2,1,0:T(8,128)(2,1)} %param.11) | copy-start | bytes 393220
  52.0 8.9 %collective-permute-start.1 = (bf16[2,8,8,128]{3,2,1,0:T(8,128)(2,1)S(1)}, bf16[2,8,8,128]{3,2,1,0:T(8,128)(2,1)S(1)}, u32[]{:S(2)}, u32[]{:S(2)}) collective-permute-start(bf16[2,8,8,128]{3,2,1,0:T(8,128)(2,1)S(1)} %get-tuple-element.17), channel_id=1, source_target_pairs={{0,128},{64,192},{128,0},{192,64},{256,384},{320,448},{384,256},{4... | collective-permute-start | bytes 98312 | tf_op jit(solution)/shard_map/ppermute | solution.py:320

commit v3 on v2

--- a/solution.py
+++ b/solution.py
@@ -44,10 +44,8 @@
     block = 2.0 * math.pi * np.outer(np.arange(BLOCK), np.arange(BLOCK)) / BLOCK
     came = slots(half, FAR_IN)
     first_high, first_low = split_table(np.concatenate([np.cos(first), -np.sin(first)], 0)[:, came])
-    last_high, last_low = split_table(
-        np.concatenate([np.cos(first).T, -np.sin(first).T], 1) * (2.0 / length)
-    )
-    back = np.concatenate([last_high, last_high, last_low], 1)
+    back = np.concatenate([np.cos(first).T, -np.sin(first).T], 1) * (2.0 / length)
+    back = back.astype(bf16)
     cos, sin = np.cos(block), np.sin(block)
     mid_high, mid_low = split_table(np.block([[cos, -sin], [sin, cos]]))
     return {
@@ -68,7 +66,7 @@
     return jnp.dot(left, right, preferred_element_type=f32)
 
 
-def middle_transform(rows, middle_ref):
+def middle_exact(rows, middle_ref):
     high, low = split(rows)
     return dot(jnp.concatenate([high, low, high], 1), middle_ref[...])
 
@@ -88,19 +86,18 @@
         re = section[:half, c * BLOCK : (c + 1) * BLOCK]
         im = section[half:, c * BLOCK : (c + 1) * BLOCK]
         rows.append(jnp.concatenate([re * cos + im * sin, im * cos - re * sin], 1))
-    return middle_transform(jnp.concatenate(rows, 0), middle_ref)
+    return middle_exact(jnp.concatenate(rows, 0), middle_ref)
 
 
 def inverse_rows(spec, chans, half, out_ref, back_ref, turn_ref, middle_ref):
-    inner = middle_transform(spec, middle_ref)
+    inner = dot(spec.astype(bf16), middle_ref[: 2 * BLOCK, :])
     cos, sin = turn_ref[0], turn_ref[1]
     cols = []
     for c in range(chans):
         re = inner[c * half : (c + 1) * half, :BLOCK]
         minus = inner[c * half : (c + 1) * half, BLOCK:]
         cols.append(jnp.concatenate([re * cos + minus * sin, re * sin - minus * cos], 0))
-    high, low = split(jnp.concatenate(cols, 1))
-    signal = dot(back_ref[...], jnp.concatenate([high, low, high], 0))
+    signal = dot(back_ref[...], jnp.concatenate(cols, 1).astype(bf16))
     for c in range(chans):
         out_ref[pl.ds(c, half, stride=chans), :] = signal[:, c * BLOCK : (c + 1) * BLOCK]
 

time: 64.1 us -> 63.2 us (0.986)
  Pallas kernels: 6.8 us -> 5.91 us
    pallas_call x7, Pallas kernels: 4.9 us -> 4.01 us  [call(): pl.pallas_call(kernel, out_shape=out, in_specs=[vmem] * (len(args) - any_...]
  transfers between devices with their start and end apart: 4 -> 4, of which waited for: 2 -> 2; matrix products, arithmetic and copies ran while one was open for 0% -> 0% of each run, Pallas kernels for 4% -> 3%
where the time goes in v3:
time: 63.2 us; the launch traced here: 62.9 us
  starting transfers between devices  42.3 us (67%)
  waiting for transfers between devices  11.7 us (19%)
  Pallas kernels  5.91 us (9%)
  blocking collectives  2.06 us (3%)
  between operations  0.84 us (1%)
    all_to_all x1, starting transfers between devices, local(): lax.all_to_all(gated, 'ctx', 0, 0, tiled=True, axis_index_groups=[slots(h...  20.4 us
    all_to_all x1, starting transfers between devices, local(): lax.all_to_all(carried, 'ctx', 0, 0, tiled=True, axis_index_groups=[slots...  14.9 us
    ppermute x1, waiting for transfers between devices, local(): other = lax.ppermute(send, 'dp', [(i, i ^ 2) for i in range(groups)])  5.96 us
    all_to_all x1, waiting for transfers between devices, local(): lax.all_to_all(gated, 'ctx', 0, 0, tiled=True, axis_index_groups=[slots(h...  5.76 us
    pallas_call x7, Pallas kernels, call(): pl.pallas_call(kernel, out_shape=out, in_specs=[vmem] * (len(args) - any_...  4.01 us
    ppermute x1, starting transfers between devices, local(): other = lax.ppermute(send, 'dp', [(i, i ^ 4) for i in range(groups)])  4.01 us
    ppermute x1, starting transfers between devices, local(): other = lax.ppermute(send, 'dp', [(i, i ^ 2) for i in range(groups)])  2.89 us
    all_gather x1, blocking collectives, local(): other = lax.all_gather(send, 'dp', axis=0, axis_index_groups=cores)  2.06 us
  transfers between devices with their start and end apart: 4, of which 2 were waited for; matrix products, arithmetic and copies ran while one was open for 0% of the time, Pallas kernels for 3%

profile of v3, /device:TPU:1, one launch (start us, length us, event | category | flops | bytes accessed | tf_op | source)
XLA Modules:
  0.0 62.9 jit_solution(18068070452038173985)
XLA Ops:
  0.6 0.0 copy-start.6
  0.6 1.9 %gate.1 = bf16[64,16,128]{2,1,0:T(8,128)(2,1)} custom-call(bf16[512,128]{1,0:T(8,128)(2,1)} %bitcast.8, bf16[512,128]{1,0:T(8,128)(2,1)} %bitcast.10, bf16[512,128]{1,0:T(8,128)(2,1)} %bitcast.12, bf16[512,128]{1,0:T(8,128)(2,1)} %bitcast.15), custom_call_target="tpu_custom_call" | custom-call | flops 131072 | bytes 786432 | tf_op jit(solution)/shard_map/gate/pallas_call | solution.py:240
  2.5 0.0 copy-start.3
  2.6 0.0 copy-start.4
  2.6 0.0 copy-start.7
  2.6 20.4 %all-to-all-start = ((bf16[64,16,128]{2,1,0:T(8,128)(2,1)}), bf16[64,16,128]{2,1,0:T(8,128)(2,1)S(1)}, u32[]{:S(2)}, u32[]{:S(2)}) async-start(bf16[64,16,128]{2,1,0:T(8,128)(2,1)} %gate.1), calls=%async_computation | async-start | bytes 524288 | tf_op jit(solution)/shard_map/all_to_all | solution.py:255
  23.0 0.0 copy-done.6
  23.1 0.0 copy-done.3
  23.1 0.0 copy-done.4
  23.1 0.0 copy-done.7
  23.1 0.6 filter.1.filter_ref
  23.6 0.0 copy-start.5
  23.7 5.8 %all-to-all-done.both_ref = bf16[64,16,128]{2,1,0:T(8,128)(2,1)S(1)} async-done(((bf16[64,16,128]{2,1,0:T(8,128)(2,1)}), bf16[64,16,128]{2,1,0:T(8,128)(2,1)S(1)}, u32[]{:S(2)}, u32[]{:S(2)}) %all-to-all-start) | async-done | bytes 262176 | tf_op jit(solution)/shard_map/all_to_all | solution.py:255
  29.4 0.9 %forward.1.spec_ref = f32[1024,256]{1,0:T(8,128)S(1)} custom-call(bf16[64,16,128]{2,1,0:T(8,128)(2,1)S(1)} %all-to-all-done.both_ref, bf16[128,192]{1,0:T(8,128)(2,1)S(1)} %copy-done.7, f32[2,64,128]{2,1,0:T(8,128)S(1)} %copy-done.4, bf16[768,256]{1,0:T(8,128)(2,1)S(1)} %copy-done.3), custom_call_target="tpu_custom_call" | custom-call | flops 603979776 | bytes 770048 | tf_op jit(solution)/shard_map/forward/pallas_call | solution.py:211
  30.3 0.0 copy-done.5
  30.3 0.0 copy-start.8
  30.3 0.4 cross.1
  30.8 4.0 %collective-permute-start = (bf16[2,2,8,8,128]{4,3,2,1,0:T(8,128)(2,1)S(1)}, bf16[2,2,8,8,128]{4,3,2,1,0:T(8,128)(2,1)S(1)}, u32[]{:S(2)}, u32[]{:S(2)}) collective-permute-start(bf16[2,2,8,8,128]{4,3,2,1,0:T(8,128)(2,1)S(1)} %get-tuple-element.14.after_ref), channel_id=1, source_target_pairs={{0,256},{64,320},{128,384},{192,448},{256,0},{320,64},{384,128},{4... | collective-permute-start | bytes 196616 | tf_op jit(solution)/shard_map/ppermute | solution.py:294
  34.8 0.0 copy-done.8
  34.8 1.3 %conv.1 = bf16[64,16,128]{2,1,0:T(8,128)(2,1)} custom-call(f32[1024,256]{1,0:T(8,128)S(1)} %forward.1.spec_ref, f32[512,256]{1,0:T(8,128)S(1)} %filter.1.filter_ref, bf16[64,128]{1,0:T(8,128)(2,1)S(1)} %copy-done.8, f32[2,64,128]{2,1,0:T(8,128)S(1)} %copy-done.4, bf16[768,256]{1,0:T(8,128)(2,1)S(1)} %copy-done.3, ...), custom_call_target="tpu_custom_call" | custom-call | flops 805306368 | bytes 2113536 | tf_op jit(solution)/shard_map/conv/pallas_call | solution.py:211
  36.1 14.9 %all-to-all-start.1 = ((bf16[64,16,128]{2,1,0:T(8,128)(2,1)}), bf16[64,16,128]{2,1,0:T(8,128)(2,1)S(1)}, u32[]{:S(2)}, u32[]{:S(2)}) async-start(bf16[64,16,128]{2,1,0:T(8,128)(2,1)} %conv.1), calls=%async_computation.1 | async-start | bytes 524288 | tf_op jit(solution)/shard_map/all_to_all | solution.py:327
  51.0 0.0 collective-permute-done.other_ref
  51.0 0.0 copy-start.1
  51.1 0.0 copy-start.2
  51.1 0.0 copy-start
  51.1 2.9 %collective-permute-start.1 = (bf16[2,8,8,128]{3,2,1,0:T(8,128)(2,1)S(1)}, bf16[2,8,8,128]{3,2,1,0:T(8,128)(2,1)S(1)}, u32[]{:S(2)}, u32[]{:S(2)}) collective-permute-start(bf16[2,8,8,128]{3,2,1,0:T(8,128)(2,1)S(1)} %get-tuple-element.17), channel_id=1, source_target_pairs={{0,128},{64,192},{128,0},{192,64},{256,384},{320,448},{384,256},{4... | collective-permute-start | bytes 98312 | tf_op jit(solution)/shard_map/ppermute | solution.py:317
  54.0 6.0 %collective-permute-done.1.other_ref = bf16[2,8,8,128]{3,2,1,0:T(8,128)(2,1)S(1)} collective-permute-done((bf16[2,8,8,128]{3,2,1,0:T(8,128)(2,1)S(1)}, bf16[2,8,8,128]{3,2,1,0:T(8,128)(2,1)S(1)}, u32[]{:S(2)}, u32[]{:S(2)}) %collective-permute-start.1) | collective-permute-done | bytes 32800 | tf_op jit(solution)/shard_map/ppermute | solution.py:317
  60.0 2.1 %all-gather = bf16[16,8,128]{2,1,0:T(8,128)(2,1)S(1)} all-gather(bf16[8,8,128]{2,1,0:T(8,128)(2,1)S(1)} %get-tuple-element.19), channel_id=2, replica_groups={{0,64},{128,192},{256,320},{384,448},{1,65},{129,193},{257,321},{385,44..., dimensions={0}, use_global_device_ids=true | all-gather | bytes 49152 | tf_op jit(solution)/shard_map/all_gather | solution.py:326
  62.0 0.0 all-to-all-done.1.both_ref
  62.1 0.0 copy-done.1
  62.1 0.0 copy-done.2
  62.1 0.0 copy-done
  62.1 0.8 %final.1 = (bf16[512,128]{1,0:T(8,128)(2,1)}, bf16[512,128]{1,0:T(8,128)(2,1)}, bf16[512,128]{1,0:T(8,128)(2,1)}, f32[8,1024]{1,0:T(8,128)}) custom-call(bf16[64,16,128]{2,1,0:T(8,128)(2,1)S(1)} %all-to-all-done.1.both_ref, bf16[512,128]{1,0:T(8,128)(2,1)S(1)} %bitcast.9, bf16[512,128]{1,0:T(8,128)(2,1)S(1)} %bitcast.11, bf16[512,128]{1,0:T(8,128)(2,1)S(1)} %bitcast.13, ...), custom_call_target="tpu_custom_call" | custom-call | bytes 720896 | tf_op jit(solution)/shard_map/final/pallas_call | solution.py:211
  (2 shorter events, 0.0 us)
Async XLA Ops:
  0.6 22.4 %copy-start.6 = (f32[8,8192]{1,0:T(8,128)S(1)}, f32[8,8192]{1,0:T(8,128)}, u32[]{:S(2)}) copy-start(f32[8,8192]{1,0:T(8,128)} %filter_ref.1) | copy-start | bytes 786436
  2.5 20.5 %copy-start.3 = (bf16[768,256]{1,0:T(8,128)(2,1)S(1)}, bf16[768,256]{1,0:T(8,128)(2,1)}, u32[]{:S(2)}) copy-start(bf16[768,256]{1,0:T(8,128)(2,1)} %constant.13.clone.middle_ref) | copy-start | bytes 1179652
  2.6 20.5 %copy-start.4 = (f32[2,64,128]{2,1,0:T(8,128)S(1)}, f32[2,64,128]{2,1,0:T(8,128)}, u32[]{:S(2)}) copy-start(f32[2,64,128]{2,1,0:T(8,128)} %constant.14.clone.turn_ref) | copy-start | bytes 196612
  2.6 20.5 %copy-start.7 = (bf16[128,192]{1,0:T(8,128)(2,1)S(1)}, bf16[128,192]{1,0:T(8,128)(2,1)}, u32[]{:S(2)}) copy-start(bf16[128,192]{1,0:T(8,128)(2,1)} %constant.10.clone.forward_ref) | copy-start | bytes 147460
  2.6 26.8 %all-to-all-start = ((bf16[64,16,128]{2,1,0:T(8,128)(2,1)}), bf16[64,16,128]{2,1,0:T(8,128)(2,1)S(1)}, u32[]{:S(2)}, u32[]{:S(2)}) async-start(bf16[64,16,128]{2,1,0:T(8,128)(2,1)} %gate.1), calls=%async_computation | async-start | bytes 524288 | tf_op jit(solution)/shard_map/all_to_all | solution.py:255
  23.6 6.6 %copy-start.5 = (bf16[64,128]{1,0:T(8,128)(2,1)S(1)}, bf16[64,128]{1,0:T(8,128)(2,1)}, u32[]{:S(2)}) copy-start(bf16[64,128]{1,0:T(8,128)(2,1)} %constant.12.clone.back_ref) | copy-start | bytes 49156
  30.3 4.5 %copy-start.8 = (bf16[64,128]{1,0:T(8,128)(2,1)S(1)}, bf16[64,128]{1,0:T(8,128)(2,1)}, u32[]{:S(2)}) copy-start(bf16[64,128]{1,0:T(8,128)(2,1)} %constant.11.clone.back_ref) | copy-start | bytes 49156
  30.8 20.3 %collective-permute-start = (bf16[2,2,8,8,128]{4,3,2,1,0:T(8,128)(2,1)S(1)}, bf16[2,2,8,8,128]{4,3,2,1,0:T(8,128)(2,1)S(1)}, u32[]{:S(2)}, u32[]{:S(2)}) collective-permute-start(bf16[2,2,8,8,128]{4,3,2,1,0:T(8,128)(2,1)S(1)} %get-tuple-element.14.after_ref), channel_id=1, source_target_pairs={{0,256},{64,320},{128,384},{192,448},{256,0},{320,64},{384,128},{4... | collective-permute-start | bytes 196616 | tf_op jit(solution)/shard_map/ppermute | solution.py:294
  36.1 25.9 %all-to-all-start.1 = ((bf16[64,16,128]{2,1,0:T(8,128)(2,1)}), bf16[64,16,128]{2,1,0:T(8,128)(2,1)S(1)}, u32[]{:S(2)}, u32[]{:S(2)}) async-start(bf16[64,16,128]{2,1,0:T(8,128)(2,1)} %conv.1), calls=%async_computation.1 | async-start | bytes 524288 | tf_op jit(solution)/shard_map/all_to_all | solution.py:327
  51.0 11.0 %copy-start.1 = (bf16[1,512,128]{2,1,0:T(8,128)(2,1)S(1)}, bf16[1,512,128]{2,1,0:T(8,128)(2,1)}, u32[]{:S(2)}) copy-start(bf16[1,512,128]{2,1,0:T(8,128)(2,1)} %param.12) | copy-start | bytes 393220
  51.1 11.0 %copy-start.2 = (bf16[1,512,128]{2,1,0:T(8,128)(2,1)S(1)}, bf16[1,512,128]{2,1,0:T(8,128)(2,1)}, u32[]{:S(2)}) copy-start(bf16[1,512,128]{2,1,0:T(8,128)(2,1)} %param.13) | copy-start | bytes 393220
  51.1 11.0 %copy-start = (bf16[1,512,128]{2,1,0:T(8,128)(2,1)S(1)}, bf16[1,512,128]{2,1,0:T(8,128)(2,1)}, u32[]{:S(2)}) copy-start(bf16[1,512,128]{2,1,0:T(8,128)(2,1)} %param.11) | copy-start | bytes 393220
  51.1 8.9 %collective-permute-start.1 = (bf16[2,8,8,128]{3,2,1,0:T(8,128)(2,1)S(1)}, bf16[2,8,8,128]{3,2,1,0:T(8,128)(2,1)S(1)}, u32[]{:S(2)}, u32[]{:S(2)}) collective-permute-start(bf16[2,8,8,128]{3,2,1,0:T(8,128)(2,1)S(1)} %get-tuple-element.17), channel_id=1, source_target_pairs={{0,128},{64,192},{128,0},{192,64},{256,384},{320,448},{384,256},{4... | collective-permute-start | bytes 98312 | tf_op jit(solution)/shard_map/ppermute | solution.py:317

commit v4 on v3

--- a/solution.py
+++ b/solution.py
@@ -149,18 +149,28 @@
     dz_re, dz_im = spec_ref[count:, :BLOCK], spec_ref[count:, BLOCK:]
     cross = jnp.concatenate([kv_re * dz_re + kv_im * dz_im, kv_im * dz_re - kv_re * dz_im], 1)
     inverse_rows(cross, chans, half, out_rows, back_ref, turn_ref, middle_ref)
-    bit = lax.div(lax.axis_index("dp"), 4)
-    size = out_rows.shape[0] // 2
-    kept = pl.multiple_of(bit * size, size)
-    sent = pl.multiple_of((1 - bit) * size, size)
-    keep_ref[...] = out_rows[pl.ds(kept, size), :].reshape(keep_ref.shape)
-    send_ref[...] = out_rows[pl.ds(sent, size), :].reshape(send_ref.shape).astype(bf16)
-
-
-def halve_kernel(keep_ref, other_ref, mine_ref, send_ref, *, axis_bit):
-    bit = lax.rem(lax.div(lax.axis_index("dp"), axis_bit), 2)
-    mine_ref[...] = keep_ref[bit] + other_ref[bit].astype(f32)
-    send_ref[...] = (keep_ref[1 - bit] + other_ref[1 - bit].astype(f32)).astype(bf16)
+    bit = lax.rem(lax.div(lax.axis_index("dp"), 2), 2)
+    size = out_rows.shape[0] // 4
+    shape = keep_ref.shape[1:]
+    for i in range(2):
+        kept = pl.multiple_of((2 * i + bit) * size, size)
+        sent = pl.multiple_of((2 * i + 1 - bit) * size, size)
+        keep_ref[i] = out_rows[pl.ds(kept, size), :].reshape(shape)
+        send_ref[i] = out_rows[pl.ds(sent, size), :].reshape(shape).astype(bf16)
+
+
+def core_kernel(keep_ref, other_ref, mine_ref, send_ref):
+    core = lax.rem(lax.axis_index("dp"), 2)
+    for i in range(2):
+        mine_ref[i] = keep_ref[i, core] + other_ref[i, core].astype(f32)
+        send_ref[i] = (keep_ref[i, 1 - core] + other_ref[i, 1 - core].astype(f32)).astype(bf16)
+
+
+def halve_kernel(keep_ref, other_ref, mine_ref, send_ref):
+    place = lax.axis_index("dp")
+    core, bit = lax.rem(place, 2), lax.div(place, 4)
+    mine_ref[...] = keep_ref[bit] + other_ref[1 - core, bit].astype(f32)
+    send_ref[...] = (keep_ref[1 - bit] + other_ref[1 - core, 1 - bit].astype(f32)).astype(bf16)
 
 
 def conv_kernel(spec_ref, filter_ref, back_ref, turn_ref, middle_ref, after_ref, out_ref, out_rows):
@@ -191,8 +201,7 @@
     *,
     scale,
 ):
-    core = lax.rem(lax.axis_index("dp"), 2)
-    lags = (keep_ref[...] + other_ref[1 - core].astype(f32)) * scale
+    lags = (keep_ref[...] + other_ref[...].astype(f32)) * scale
     for a in range(lags.shape[0]):
         gf_ref[:, a * BLOCK : (a + 1) * BLOCK] = lags[a]
     groups, both, _ = both_ref.shape
@@ -291,7 +300,7 @@
         flops=2 * work,
         name="cross",
     )
-    other = lax.ppermute(send, "dp", [(i, i ^ 4) for i in range(groups)])
+    other = lax.ppermute(send, "dp", [(i, i ^ 2) for i in range(groups)])
     carried = call(
         conv_kernel,
         pieces,
@@ -307,23 +316,23 @@
         name="conv",
     )
     keep, send = call(
-        functools.partial(halve_kernel, axis_bit=2),
+        core_kernel,
         (shape((2, *quad), f32), shape((2, *quad), bf16)),
         keep,
         other,
         flops=HINT,
-        name="halve",
-    )
-    other = lax.ppermute(send, "dp", [(i, i ^ 2) for i in range(groups)])
+        name="core",
+    )
+    cores = [[2 * z, 2 * z + 1] for z in range(quads)]
+    other = lax.all_gather(send, "dp", axis=0, axis_index_groups=cores)
     keep, send = call(
-        functools.partial(halve_kernel, axis_bit=1),
+        halve_kernel,
         (shape(quad, f32), shape(quad, bf16)),
         keep,
         other,
-        name="pair",
-    )
-    cores = [[2 * z, 2 * z + 1] for z in range(quads)]
-    other = lax.all_gather(send, "dp", axis=0, axis_index_groups=cores)
+        name="halve",
+    )
+    other = lax.ppermute(send, "dp", [(i, i ^ 4) for i in range(groups)])
     back_here = lax.all_to_all(
         carried, "ctx", 0, 0, tiled=True, axis_index_groups=[slots(half, FAR_OUT)]
     )

time: 63.2 us -> 60.9 us (0.964)
  waiting for transfers between devices: 11.7 us -> 7.37 us
  blocking collectives: 2.06 us -> 4.23 us
    ppermute x1, waiting for transfers between devices: 5.96 us -> 0.01 us  [local(): other = lax.ppermute(send, 'dp', [(i, i ^ 2) for i in range(groups)])]
    all_gather x1, blocking collectives: 2.06 us -> 4.23 us  [local(): other = lax.all_gather(send, 'dp', axis=0, axis_index_groups=cores)]
    ppermute x1, waiting for transfers between devices: 0.01 us -> 1.61 us  [local(): other = lax.ppermute(send, 'dp', [(i, i ^ 4) for i in range(groups)])]
where the time goes in v4:
time: 60.9 us; the launch traced here: 60.5 us
  starting transfers between devices  42.1 us (69%)
  waiting for transfers between devices  7.37 us (12%)
  Pallas kernels  5.92 us (10%)
  blocking collectives  4.23 us (7%)
  between operations  0.84 us (1%)
    all_to_all x1, starting transfers between devices, local(): lax.all_to_all(gated, 'ctx', 0, 0, tiled=True, axis_index_groups=[slots(h...  20.4 us
    all_to_all x1, starting transfers between devices, local(): lax.all_to_all(carried, 'ctx', 0, 0, tiled=True, axis_index_groups=[slots...  14.6 us
    all_to_all x1, waiting for transfers between devices, local(): lax.all_to_all(gated, 'ctx', 0, 0, tiled=True, axis_index_groups=[slots(h...  5.76 us
    all_gather x1, blocking collectives, local(): other = lax.all_gather(send, 'dp', axis=0, axis_index_groups=cores)  4.23 us
    pallas_call x7, Pallas kernels, call(): pl.pallas_call(kernel, out_shape=out, in_specs=[vmem] * (len(args) - any_...  4.02 us
    ppermute x1, starting transfers between devices, local(): other = lax.ppermute(send, 'dp', [(i, i ^ 4) for i in range(groups)])  4 us
    ppermute x1, starting transfers between devices, local(): other = lax.ppermute(send, 'dp', [(i, i ^ 2) for i in range(groups)])  3.1 us
    pallas_call x1, Pallas kernels, local(): pl.pallas_call(gate_kernel, out_shape=pieces, in_specs=[pl.BlockSpec(memo...  1.9 us
  transfers between devices with their start and end apart: 4, of which 2 were waited for; matrix products, arithmetic and copies ran while one was open for 0% of the time, Pallas kernels for 3%

profile of v4, /device:TPU:1, one launch (start us, length us, event | category | flops | bytes accessed | tf_op | source)
XLA Modules:
  0.0 60.5 jit_solution(10211466392924014835)
XLA Ops:
  0.6 0.0 copy-start.6
  0.6 1.9 %gate.1 = bf16[64,16,128]{2,1,0:T(8,128)(2,1)} custom-call(bf16[512,128]{1,0:T(8,128)(2,1)} %bitcast.8, bf16[512,128]{1,0:T(8,128)(2,1)} %bitcast.10, bf16[512,128]{1,0:T(8,128)(2,1)} %bitcast.12, bf16[512,128]{1,0:T(8,128)(2,1)} %bitcast.15), custom_call_target="tpu_custom_call" | custom-call | flops 131072 | bytes 786432 | tf_op jit(solution)/shard_map/gate/pallas_call | solution.py:249
  2.5 0.0 copy-start.3
  2.6 0.0 copy-start.4
  2.6 0.0 copy-start.7
  2.6 20.4 %all-to-all-start = ((bf16[64,16,128]{2,1,0:T(8,128)(2,1)}), bf16[64,16,128]{2,1,0:T(8,128)(2,1)S(1)}, u32[]{:S(2)}, u32[]{:S(2)}) async-start(bf16[64,16,128]{2,1,0:T(8,128)(2,1)} %gate.1), calls=%async_computation | async-start | bytes 524288 | tf_op jit(solution)/shard_map/all_to_all | solution.py:264
  23.0 0.0 copy-done.6
  23.1 0.0 copy-done.3
  23.1 0.0 copy-done.4
  23.1 0.0 copy-done.7
  23.1 0.6 filter.1.filter_ref
  23.6 0.0 copy-start.5
  23.7 5.8 %all-to-all-done.both_ref = bf16[64,16,128]{2,1,0:T(8,128)(2,1)S(1)} async-done(((bf16[64,16,128]{2,1,0:T(8,128)(2,1)}), bf16[64,16,128]{2,1,0:T(8,128)(2,1)S(1)}, u32[]{:S(2)}, u32[]{:S(2)}) %all-to-all-start) | async-done | bytes 262176 | tf_op jit(solution)/shard_map/all_to_all | solution.py:264
  29.4 0.9 %forward.1.spec_ref = f32[1024,256]{1,0:T(8,128)S(1)} custom-call(bf16[64,16,128]{2,1,0:T(8,128)(2,1)S(1)} %all-to-all-done.both_ref, bf16[128,192]{1,0:T(8,128)(2,1)S(1)} %copy-done.7, f32[2,64,128]{2,1,0:T(8,128)S(1)} %copy-done.4, bf16[768,256]{1,0:T(8,128)(2,1)S(1)} %copy-done.3), custom_call_target="tpu_custom_call" | custom-call | flops 603979776 | bytes 770048 | tf_op jit(solution)/shard_map/forward/pallas_call | solution.py:220
  30.3 0.0 copy-done.5
  30.3 0.0 copy-start.8
  30.3 0.5 cross.1
  30.8 3.1 %collective-permute-start = (bf16[2,2,8,8,128]{4,3,2,1,0:T(8,128)(2,1)S(1)}, bf16[2,2,8,8,128]{4,3,2,1,0:T(8,128)(2,1)S(1)}, u32[]{:S(2)}, u32[]{:S(2)}) collective-permute-start(bf16[2,2,8,8,128]{4,3,2,1,0:T(8,128)(2,1)S(1)} %get-tuple-element.14.after_ref), channel_id=1, source_target_pairs={{0,128},{64,192},{128,0},{192,64},{256,384},{320,448},{384,256},{4... | collective-permute-start | bytes 196616 | tf_op jit(solution)/shard_map/ppermute | solution.py:303
  33.9 0.0 copy-done.8
  33.9 1.3 %conv.1 = bf16[64,16,128]{2,1,0:T(8,128)(2,1)} custom-call(f32[1024,256]{1,0:T(8,128)S(1)} %forward.1.spec_ref, f32[512,256]{1,0:T(8,128)S(1)} %filter.1.filter_ref, bf16[64,128]{1,0:T(8,128)(2,1)S(1)} %copy-done.8, f32[2,64,128]{2,1,0:T(8,128)S(1)} %copy-done.4, bf16[768,256]{1,0:T(8,128)(2,1)S(1)} %copy-done.3, ...), custom_call_target="tpu_custom_call" | custom-call | flops 805306368 | bytes 2113536 | tf_op jit(solution)/shard_map/conv/pallas_call | solution.py:220
  35.2 14.6 %all-to-all-start.1 = ((bf16[64,16,128]{2,1,0:T(8,128)(2,1)}), bf16[64,16,128]{2,1,0:T(8,128)(2,1)S(1)}, u32[]{:S(2)}, u32[]{:S(2)}) async-start(bf16[64,16,128]{2,1,0:T(8,128)(2,1)} %conv.1), calls=%async_computation.1 | async-start | bytes 524288 | tf_op jit(solution)/shard_map/all_to_all | solution.py:336
  49.8 0.0 collective-permute-done.other_ref
  49.8 0.0 copy-start.1
  49.8 0.0 copy-start.2
  49.9 0.0 copy-start
  49.9 4.2 %all-gather = bf16[4,8,8,128]{3,2,1,0:T(8,128)(2,1)S(1)} all-gather(bf16[2,8,8,128]{3,2,1,0:T(8,128)(2,1)S(1)} %get-tuple-element.17), channel_id=2, replica_groups={{0,64},{128,192},{256,320},{384,448},{1,65},{129,193},{257,321},{385,44..., dimensions={0}, use_global_device_ids=true | all-gather | bytes 98304 | tf_op jit(solution)/shard_map/all_gather | solution.py:327
  54.1 4.0 %collective-permute-start.1 = (bf16[8,8,128]{2,1,0:T(8,128)(2,1)S(1)}, bf16[8,8,128]{2,1,0:T(8,128)(2,1)S(1)}, u32[]{:S(2)}, u32[]{:S(2)}) collective-permute-start(bf16[8,8,128]{2,1,0:T(8,128)(2,1)S(1)} %get-tuple-element.19), channel_id=1, source_target_pairs={{0,256},{64,320},{128,384},{192,448},{256,0},{320,64},{384,128},{4... | collective-permute-start | bytes 49160 | tf_op jit(solution)/shard_map/ppermute | solution.py:335
  58.1 1.6 %collective-permute-done.1.other_ref = bf16[8,8,128]{2,1,0:T(8,128)(2,1)S(1)} collective-permute-done((bf16[8,8,128]{2,1,0:T(8,128)(2,1)S(1)}, bf16[8,8,128]{2,1,0:T(8,128)(2,1)S(1)}, u32[]{:S(2)}, u32[]{:S(2)}) %collective-permute-start.1) | collective-permute-done | bytes 16416 | tf_op jit(solution)/shard_map/ppermute | solution.py:335
  59.7 0.0 all-to-all-done.1.both_ref
  59.7 0.0 copy-done.1
  59.7 0.0 copy-done.2
  59.7 0.0 copy-done
  59.7 0.8 %final.1 = (bf16[512,128]{1,0:T(8,128)(2,1)}, bf16[512,128]{1,0:T(8,128)(2,1)}, bf16[512,128]{1,0:T(8,128)(2,1)}, f32[8,1024]{1,0:T(8,128)}) custom-call(bf16[64,16,128]{2,1,0:T(8,128)(2,1)S(1)} %all-to-all-done.1.both_ref, bf16[512,128]{1,0:T(8,128)(2,1)S(1)} %bitcast.9, bf16[512,128]{1,0:T(8,128)(2,1)S(1)} %bitcast.11, bf16[512,128]{1,0:T(8,128)(2,1)S(1)} %bitcast.13, ...), custom_call_target="tpu_custom_call" | custom-call | bytes 704512 | tf_op jit(solution)/shard_map/final/pallas_call | solution.py:220
  (2 shorter events, 0.0 us)
Async XLA Ops:
  0.6 22.4 %copy-start.6 = (f32[8,8192]{1,0:T(8,128)S(1)}, f32[8,8192]{1,0:T(8,128)}, u32[]{:S(2)}) copy-start(f32[8,8192]{1,0:T(8,128)} %filter_ref.1) | copy-start | bytes 786436
  2.5 20.5 %copy-start.3 = (bf16[768,256]{1,0:T(8,128)(2,1)S(1)}, bf16[768,256]{1,0:T(8,128)(2,1)}, u32[]{:S(2)}) copy-start(bf16[768,256]{1,0:T(8,128)(2,1)} %constant.13.clone.middle_ref) | copy-start | bytes 1179652
  2.6 20.5 %copy-start.4 = (f32[2,64,128]{2,1,0:T(8,128)S(1)}, f32[2,64,128]{2,1,0:T(8,128)}, u32[]{:S(2)}) copy-start(f32[2,64,128]{2,1,0:T(8,128)} %constant.14.clone.turn_ref) | copy-start | bytes 196612
  2.6 20.5 %copy-start.7 = (bf16[128,192]{1,0:T(8,128)(2,1)S(1)}, bf16[128,192]{1,0:T(8,128)(2,1)}, u32[]{:S(2)}) copy-start(bf16[128,192]{1,0:T(8,128)(2,1)} %constant.10.clone.forward_ref) | copy-start | bytes 147460
  2.6 26.8 %all-to-all-start = ((bf16[64,16,128]{2,1,0:T(8,128)(2,1)}), bf16[64,16,128]{2,1,0:T(8,128)(2,1)S(1)}, u32[]{:S(2)}, u32[]{:S(2)}) async-start(bf16[64,16,128]{2,1,0:T(8,128)(2,1)} %gate.1), calls=%async_computation | async-start | bytes 524288 | tf_op jit(solution)/shard_map/all_to_all | solution.py:264
  23.6 6.6 %copy-start.5 = (bf16[64,128]{1,0:T(8,128)(2,1)S(1)}, bf16[64,128]{1,0:T(8,128)(2,1)}, u32[]{:S(2)}) copy-start(bf16[64,128]{1,0:T(8,128)(2,1)} %constant.12.clone.back_ref) | copy-start | bytes 49156
  30.3 3.6 %copy-start.8 = (bf16[64,128]{1,0:T(8,128)(2,1)S(1)}, bf16[64,128]{1,0:T(8,128)(2,1)}, u32[]{:S(2)}) copy-start(bf16[64,128]{1,0:T(8,128)(2,1)} %constant.11.clone.back_ref) | copy-start | bytes 49156
  30.8 19.0 %collective-permute-start = (bf16[2,2,8,8,128]{4,3,2,1,0:T(8,128)(2,1)S(1)}, bf16[2,2,8,8,128]{4,3,2,1,0:T(8,128)(2,1)S(1)}, u32[]{:S(2)}, u32[]{:S(2)}) collective-permute-start(bf16[2,2,8,8,128]{4,3,2,1,0:T(8,128)(2,1)S(1)} %get-tuple-element.14.after_ref), channel_id=1, source_target_pairs={{0,128},{64,192},{128,0},{192,64},{256,384},{320,448},{384,256},{4... | collective-permute-start | bytes 196616 | tf_op jit(solution)/shard_map/ppermute | solution.py:303
  35.2 24.5 %all-to-all-start.1 = ((bf16[64,16,128]{2,1,0:T(8,128)(2,1)}), bf16[64,16,128]{2,1,0:T(8,128)(2,1)S(1)}, u32[]{:S(2)}, u32[]{:S(2)}) async-start(bf16[64,16,128]{2,1,0:T(8,128)(2,1)} %conv.1), calls=%async_computation.1 | async-start | bytes 524288 | tf_op jit(solution)/shard_map/all_to_all | solution.py:336
  49.8 9.9 %copy-start.1 = (bf16[1,512,128]{2,1,0:T(8,128)(2,1)S(1)}, bf16[1,512,128]{2,1,0:T(8,128)(2,1)}, u32[]{:S(2)}) copy-start(bf16[1,512,128]{2,1,0:T(8,128)(2,1)} %param.12) | copy-start | bytes 393220
  49.8 9.9 %copy-start.2 = (bf16[1,512,128]{2,1,0:T(8,128)(2,1)S(1)}, bf16[1,512,128]{2,1,0:T(8,128)(2,1)}, u32[]{:S(2)}) copy-start(bf16[1,512,128]{2,1,0:T(8,128)(2,1)} %param.13) | copy-start | bytes 393220
  49.9 9.9 %copy-start = (bf16[1,512,128]{2,1,0:T(8,128)(2,1)S(1)}, bf16[1,512,128]{2,1,0:T(8,128)(2,1)}, u32[]{:S(2)}) copy-start(bf16[1,512,128]{2,1,0:T(8,128)(2,1)} %param.11) | copy-start | bytes 393220
  54.1 5.6 %collective-permute-start.1 = (bf16[8,8,128]{2,1,0:T(8,128)(2,1)S(1)}, bf16[8,8,128]{2,1,0:T(8,128)(2,1)S(1)}, u32[]{:S(2)}, u32[]{:S(2)}) collective-permute-start(bf16[8,8,128]{2,1,0:T(8,128)(2,1)S(1)} %get-tuple-element.19), channel_id=1, source_target_pairs={{0,256},{64,320},{128,384},{192,448},{256,0},{320,64},{384,128},{4... | collective-permute-start | bytes 49160 | tf_op jit(solution)/shard_map/ppermute | solution.py:335

commit v5 on v4

--- a/solution.py
+++ b/solution.py
@@ -201,7 +201,8 @@
     *,
     scale,
 ):
-    lags = (keep_ref[...] + other_ref[...].astype(f32)) * scale
+    side = lax.div(lax.axis_index("dp"), 4)
+    lags = (keep_ref[...] + other_ref[1 - side].astype(f32)) * scale
     for a in range(lags.shape[0]):
         gf_ref[:, a * BLOCK : (a + 1) * BLOCK] = lags[a]
     groups, both, _ = both_ref.shape
@@ -332,7 +333,8 @@
         other,
         name="halve",
     )
-    other = lax.ppermute(send, "dp", [(i, i ^ 4) for i in range(groups)])
+    sides = [[i, i + 4] for i in range(groups // 2)]
+    other = lax.all_gather(send, "dp", axis=0, axis_index_groups=sides)
     back_here = lax.all_to_all(
         carried, "ctx", 0, 0, tiled=True, axis_index_groups=[slots(half, FAR_OUT)]
     )

time: 60.9 us -> 59.8 us (0.982)
  blocking collectives: 4.23 us -> 8.81 us
  starting transfers between devices: 42.1 us -> 38.1 us
  waiting for transfers between devices: 7.37 us -> 5.76 us
    all_gather x0 -> x1, blocking collectives: none -> 4.58 us  [local(): other = lax.all_gather(send, 'dp', axis=0, axis_index_groups=sides)]
    ppermute x1 -> x0, starting transfers between devices: 4 us -> none  [local(): other = lax.ppermute(send, 'dp', [(i, i ^ 4) for i in range(groups)])]
    ppermute x1 -> x0, waiting for transfers between devices: 1.61 us -> none  [local(): other = lax.ppermute(send, 'dp', [(i, i ^ 4) for i in range(groups)])]
  transfers between devices with their start and end apart: 4 -> 3, of which waited for: 2 -> 1; matrix products, arithmetic and copies ran while one was open for 0% -> 0% of each run, Pallas kernels for 3% -> 3%
where the time goes in v5:
time: 59.8 us; the launch traced here: 59.5 us
  starting transfers between devices  38.1 us (64%)
  blocking collectives  8.81 us (15%)
  Pallas kernels  5.88 us (10%)
  waiting for transfers between devices  5.76 us (10%)
  between operations  0.84 us (1%)
    all_to_all x1, starting transfers between devices, local(): lax.all_to_all(gated, 'ctx', 0, 0, tiled=True, axis_index_groups=[slots(h...  20.4 us
    all_to_all x1, starting transfers between devices, local(): lax.all_to_all(carried, 'ctx', 0, 0, tiled=True, axis_index_groups=[slots...  14.6 us
    all_to_all x1, waiting for transfers between devices, local(): lax.all_to_all(gated, 'ctx', 0, 0, tiled=True, axis_index_groups=[slots(h...  5.76 us
    all_gather x1, blocking collectives, local(): other = lax.all_gather(send, 'dp', axis=0, axis_index_groups=sides)  4.58 us
    all_gather x1, blocking collectives, local(): other = lax.all_gather(send, 'dp', axis=0, axis_index_groups=cores)  4.23 us
    pallas_call x7, Pallas kernels, call(): pl.pallas_call(kernel, out_shape=out, in_specs=[vmem] * (len(args) - any_...  4 us
    ppermute x1, starting transfers between devices, local(): other = lax.ppermute(send, 'dp', [(i, i ^ 2) for i in range(groups)])  3.1 us
    pallas_call x1, Pallas kernels, local(): pl.pallas_call(gate_kernel, out_shape=pieces, in_specs=[pl.BlockSpec(memo...  1.88 us
  transfers between devices with their start and end apart: 3, of which 1 were waited for; matrix products, arithmetic and copies ran while one was open for 0% of the time, Pallas kernels for 3%

profile of v5, /device:TPU:1, one launch (start us, length us, event | category | flops | bytes accessed | tf_op | source)
XLA Modules:
  0.0 59.5 jit_solution(14710953196534505250)
XLA Ops:
  0.6 0.0 copy-start.6
  0.6 1.9 %gate.1 = bf16[64,16,128]{2,1,0:T(8,128)(2,1)} custom-call(bf16[512,128]{1,0:T(8,128)(2,1)} %bitcast.9, bf16[512,128]{1,0:T(8,128)(2,1)} %bitcast.11, bf16[512,128]{1,0:T(8,128)(2,1)} %bitcast.13, bf16[512,128]{1,0:T(8,128)(2,1)} %bitcast.17), custom_call_target="tpu_custom_call" | custom-call | flops 131072 | bytes 786432 | tf_op jit(solution)/shard_map/gate/pallas_call | solution.py:250
  2.5 0.0 copy-start.3
  2.5 0.0 copy-start.4
  2.6 0.0 copy-start.7
  2.6 20.4 %all-to-all-start = ((bf16[64,16,128]{2,1,0:T(8,128)(2,1)}), bf16[64,16,128]{2,1,0:T(8,128)(2,1)S(1)}, u32[]{:S(2)}, u32[]{:S(2)}) async-start(bf16[64,16,128]{2,1,0:T(8,128)(2,1)} %gate.1), calls=%async_computation | async-start | bytes 524288 | tf_op jit(solution)/shard_map/all_to_all | solution.py:265
  23.0 0.0 copy-done.6
  23.0 0.0 copy-done.3
  23.0 0.0 copy-done.4
  23.1 0.0 copy-done.7
  23.1 0.6 filter.1.filter_ref
  23.6 0.0 copy-start.5
  23.6 5.8 %all-to-all-done.both_ref = bf16[64,16,128]{2,1,0:T(8,128)(2,1)S(1)} async-done(((bf16[64,16,128]{2,1,0:T(8,128)(2,1)}), bf16[64,16,128]{2,1,0:T(8,128)(2,1)S(1)}, u32[]{:S(2)}, u32[]{:S(2)}) %all-to-all-start) | async-done | bytes 262176 | tf_op jit(solution)/shard_map/all_to_all | solution.py:265
  29.4 0.9 %forward.1.spec_ref = f32[1024,256]{1,0:T(8,128)S(1)} custom-call(bf16[64,16,128]{2,1,0:T(8,128)(2,1)S(1)} %all-to-all-done.both_ref, bf16[128,192]{1,0:T(8,128)(2,1)S(1)} %copy-done.7, f32[2,64,128]{2,1,0:T(8,128)S(1)} %copy-done.4, bf16[768,256]{1,0:T(8,128)(2,1)S(1)} %copy-done.3), custom_call_target="tpu_custom_call" | custom-call | flops 603979776 | bytes 770048 | tf_op jit(solution)/shard_map/forward/pallas_call | solution.py:221
  30.3 0.0 copy-done.5
  30.3 0.0 copy-start.8
  30.3 0.5 cross.1
  30.8 3.1 %collective-permute-start = (bf16[2,2,8,8,128]{4,3,2,1,0:T(8,128)(2,1)S(1)}, bf16[2,2,8,8,128]{4,3,2,1,0:T(8,128)(2,1)S(1)}, u32[]{:S(2)}, u32[]{:S(2)}) collective-permute-start(bf16[2,2,8,8,128]{4,3,2,1,0:T(8,128)(2,1)S(1)} %get-tuple-element.14.after_ref), channel_id=1, source_target_pairs={{0,128},{64,192},{128,0},{192,64},{256,384},{320,448},{384,256},{4... | collective-permute-start | bytes 196616 | tf_op jit(solution)/shard_map/ppermute | solution.py:304
  33.9 0.0 copy-done.8
  33.9 1.3 %conv.1 = bf16[64,16,128]{2,1,0:T(8,128)(2,1)} custom-call(f32[1024,256]{1,0:T(8,128)S(1)} %forward.1.spec_ref, f32[512,256]{1,0:T(8,128)S(1)} %filter.1.filter_ref, bf16[64,128]{1,0:T(8,128)(2,1)S(1)} %copy-done.8, f32[2,64,128]{2,1,0:T(8,128)S(1)} %copy-done.4, bf16[768,256]{1,0:T(8,128)(2,1)S(1)} %copy-done.3, ...), custom_call_target="tpu_custom_call" | custom-call | flops 805306368 | bytes 2113536 | tf_op jit(solution)/shard_map/conv/pallas_call | solution.py:221
  35.2 14.6 %all-to-all-start.1 = ((bf16[64,16,128]{2,1,0:T(8,128)(2,1)}), bf16[64,16,128]{2,1,0:T(8,128)(2,1)S(1)}, u32[]{:S(2)}, u32[]{:S(2)}) async-start(bf16[64,16,128]{2,1,0:T(8,128)(2,1)} %conv.1), calls=%async_computation.1 | async-start | bytes 524288 | tf_op jit(solution)/shard_map/all_to_all | solution.py:338
  49.8 0.0 collective-permute-done.other_ref
  49.8 0.0 copy-start.2
  49.8 0.0 copy-start
  49.8 0.0 copy-start.1
  49.8 4.2 %all-gather = bf16[4,8,8,128]{3,2,1,0:T(8,128)(2,1)S(1)} all-gather(bf16[2,8,8,128]{3,2,1,0:T(8,128)(2,1)S(1)} %get-tuple-element.17), channel_id=2, replica_groups={{0,64},{128,192},{256,320},{384,448},{1,65},{129,193},{257,321},{385,44..., dimensions={0}, use_global_device_ids=true | all-gather | bytes 98304 | tf_op jit(solution)/shard_map/all_gather | solution.py:328
  54.1 4.6 %all-gather.1 = bf16[16,8,128]{2,1,0:T(8,128)(2,1)S(1)} all-gather(bf16[8,8,128]{2,1,0:T(8,128)(2,1)S(1)} %get-tuple-element.19), channel_id=3, replica_groups={{0,256},{64,320},{128,384},{192,448},{1,257},{65,321},{129,385},{193,44..., dimensions={0}, use_global_device_ids=true | all-gather | bytes 49152 | tf_op jit(solution)/shard_map/all_gather | solution.py:337
  58.7 0.0 all-to-all-done.1.both_ref
  58.7 0.0 copy-done.2
  58.7 0.0 copy-done
  58.7 0.0 copy-done.1
  58.7 0.8 %final.1 = (bf16[512,128]{1,0:T(8,128)(2,1)}, bf16[512,128]{1,0:T(8,128)(2,1)}, bf16[512,128]{1,0:T(8,128)(2,1)}, f32[8,1024]{1,0:T(8,128)}) custom-call(bf16[64,16,128]{2,1,0:T(8,128)(2,1)S(1)} %all-to-all-done.1.both_ref, bf16[512,128]{1,0:T(8,128)(2,1)S(1)} %bitcast.10, bf16[512,128]{1,0:T(8,128)(2,1)S(1)} %bitcast.12, bf16[512,128]{1,0:T(8,128)(2,1)S(1)} %bitcast.14, ...), custom_call_target="tpu_custom_call" | custom-call | bytes 720896 | tf_op jit(solution)/shard_map/final/pallas_call | solution.py:221
  (2 shorter events, 0.0 us)
Async XLA Ops:
  0.6 22.4 %copy-start.6 = (f32[8,8192]{1,0:T(8,128)S(1)}, f32[8,8192]{1,0:T(8,128)}, u32[]{:S(2)}) copy-start(f32[8,8192]{1,0:T(8,128)} %filter_ref.1) | copy-start | bytes 786436
  2.5 20.5 %copy-start.3 = (bf16[768,256]{1,0:T(8,128)(2,1)S(1)}, bf16[768,256]{1,0:T(8,128)(2,1)}, u32[]{:S(2)}) copy-start(bf16[768,256]{1,0:T(8,128)(2,1)} %constant.13.clone.middle_ref) | copy-start | bytes 1179652
  2.5 20.5 %copy-start.4 = (f32[2,64,128]{2,1,0:T(8,128)S(1)}, f32[2,64,128]{2,1,0:T(8,128)}, u32[]{:S(2)}) copy-start(f32[2,64,128]{2,1,0:T(8,128)} %constant.14.clone.turn_ref) | copy-start | bytes 196612
  2.6 20.5 %copy-start.7 = (bf16[128,192]{1,0:T(8,128)(2,1)S(1)}, bf16[128,192]{1,0:T(8,128)(2,1)}, u32[]{:S(2)}) copy-start(bf16[128,192]{1,0:T(8,128)(2,1)} %constant.10.clone.forward_ref) | copy-start | bytes 147460
  2.6 26.8 %all-to-all-start = ((bf16[64,16,128]{2,1,0:T(8,128)(2,1)}), bf16[64,16,128]{2,1,0:T(8,128)(2,1)S(1)}, u32[]{:S(2)}, u32[]{:S(2)}) async-start(bf16[64,16,128]{2,1,0:T(8,128)(2,1)} %gate.1), calls=%async_computation | async-start | bytes 524288 | tf_op jit(solution)/shard_map/all_to_all | solution.py:265
  23.6 6.6 %copy-start.5 = (bf16[64,128]{1,0:T(8,128)(2,1)S(1)}, bf16[64,128]{1,0:T(8,128)(2,1)}, u32[]{:S(2)}) copy-start(bf16[64,128]{1,0:T(8,128)(2,1)} %constant.12.clone.back_ref) | copy-start | bytes 49156
  30.3 3.6 %copy-start.8 = (bf16[64,128]{1,0:T(8,128)(2,1)S(1)}, bf16[64,128]{1,0:T(8,128)(2,1)}, u32[]{:S(2)}) copy-start(bf16[64,128]{1,0:T(8,128)(2,1)} %constant.11.clone.back_ref) | copy-start | bytes 49156
  30.8 19.0 %collective-permute-start = (bf16[2,2,8,8,128]{4,3,2,1,0:T(8,128)(2,1)S(1)}, bf16[2,2,8,8,128]{4,3,2,1,0:T(8,128)(2,1)S(1)}, u32[]{:S(2)}, u32[]{:S(2)}) collective-permute-start(bf16[2,2,8,8,128]{4,3,2,1,0:T(8,128)(2,1)S(1)} %get-tuple-element.14.after_ref), channel_id=1, source_target_pairs={{0,128},{64,192},{128,0},{192,64},{256,384},{320,448},{384,256},{4... | collective-permute-start | bytes 196616 | tf_op jit(solution)/shard_map/ppermute | solution.py:304
  35.2 23.5 %all-to-all-start.1 = ((bf16[64,16,128]{2,1,0:T(8,128)(2,1)}), bf16[64,16,128]{2,1,0:T(8,128)(2,1)S(1)}, u32[]{:S(2)}, u32[]{:S(2)}) async-start(bf16[64,16,128]{2,1,0:T(8,128)(2,1)} %conv.1), calls=%async_computation.1 | async-start | bytes 524288 | tf_op jit(solution)/shard_map/all_to_all | solution.py:338
  49.8 8.9 %copy-start.2 = (bf16[1,512,128]{2,1,0:T(8,128)(2,1)S(1)}, bf16[1,512,128]{2,1,0:T(8,128)(2,1)}, u32[]{:S(2)}) copy-start(bf16[1,512,128]{2,1,0:T(8,128)(2,1)} %param.13) | copy-start | bytes 393220
  49.8 8.9 %copy-start = (bf16[1,512,128]{2,1,0:T(8,128)(2,1)S(1)}, bf16[1,512,128]{2,1,0:T(8,128)(2,1)}, u32[]{:S(2)}) copy-start(bf16[1,512,128]{2,1,0:T(8,128)(2,1)} %param.11) | copy-start | bytes 393220
  49.8 8.9 %copy-start.1 = (bf16[1,512,128]{2,1,0:T(8,128)(2,1)S(1)}, bf16[1,512,128]{2,1,0:T(8,128)(2,1)}, u32[]{:S(2)}) copy-start(bf16[1,512,128]{2,1,0:T(8,128)(2,1)} %param.12) | copy-start | bytes 393220

commit v6 on v5

--- a/solution.py
+++ b/solution.py
@@ -86,7 +86,10 @@
         re = section[:half, c * BLOCK : (c + 1) * BLOCK]
         im = section[half:, c * BLOCK : (c + 1) * BLOCK]
         rows.append(jnp.concatenate([re * cos + im * sin, im * cos - re * sin], 1))
-    return middle_exact(jnp.concatenate(rows, 0), middle_ref)
+    rows = jnp.concatenate(rows, 0)
+    if exact:
+        return dot(rows.astype(bf16), middle_ref[: 2 * BLOCK, :])
+    return middle_exact(rows, middle_ref)
 
 
 def inverse_rows(spec, chans, half, out_ref, back_ref, turn_ref, middle_ref):
@@ -135,13 +138,7 @@
     spec_ref[...] = forward_rows(rows, chans, half, False, forward_ref, turn_ref, middle_ref)
 
 
-def forward_kernel(both_ref, forward_ref, turn_ref, middle_ref, spec_ref, rows):
-    half, both, _ = both_ref.shape
-    rows[...] = both_ref[...].astype(f32).reshape(half * both, BLOCK)
-    spec_ref[...] = forward_rows(rows, both, half, True, forward_ref, turn_ref, middle_ref)
-
-
-def cross_kernel(spec_ref, back_ref, turn_ref, middle_ref, keep_ref, send_ref, out_rows):
+def cross_terms(spec_ref, back_ref, turn_ref, middle_ref, keep_ref, send_ref, out_rows):
     pairs, cores, own, chans, _ = keep_ref.shape
     half = 2 * pairs * cores * own
     count = chans * half
@@ -173,8 +170,26 @@
     send_ref[...] = (keep_ref[1 - bit] + other_ref[1 - core, 1 - bit].astype(f32)).astype(bf16)
 
 
-def conv_kernel(spec_ref, filter_ref, back_ref, turn_ref, middle_ref, after_ref, out_ref, out_rows):
-    half, both, _ = out_ref.shape
+def transform_kernel(
+    both_ref,
+    filter_ref,
+    forward_ref,
+    back_ref,
+    lag_ref,
+    turn_ref,
+    middle_ref,
+    out_hbm,
+    keep_ref,
+    send_ref,
+    spec_ref,
+    out_rows,
+    lag_rows,
+    made,
+    sem,
+):
+    half, both, _ = out_hbm.shape
+    out_rows[...] = both_ref[...].astype(f32).reshape(half * both, BLOCK)
+    spec_ref[...] = forward_rows(out_rows, both, half, True, forward_ref, turn_ref, middle_ref)
     count = half * both // 2
     f_re, f_im = filter_ref[:, :BLOCK], filter_ref[:, BLOCK:]
     kv_re, kv_im = spec_ref[:count, :BLOCK], spec_ref[:count, BLOCK:]
@@ -184,7 +199,11 @@
     inverse_rows(
         jnp.concatenate([conv, dkv], 0), both, half, out_rows, back_ref, turn_ref, middle_ref
     )
-    out_ref[...] = out_rows[...].reshape(half, both, BLOCK).astype(bf16)
+    made[...] = out_rows[...].reshape(half, both, BLOCK).astype(bf16)
+    done = pltpu.make_async_copy(made, out_hbm, sem)
+    done.start()
+    cross_terms(spec_ref, lag_ref, turn_ref, middle_ref, keep_ref, send_ref, lag_rows)
+    done.wait()
 
 
 def final_kernel(
@@ -276,46 +295,27 @@
         flops=2 * work,
         name="filter",
     )
-    spec = call(
-        forward_kernel,
-        shape((both * half, 2 * BLOCK), f32),
-        here,
-        forward,
-        turn,
-        middle,
-        scratch=[(half * both, BLOCK)],
-        flops=3 * work,
-        name="forward",
-    )
     own = half // groups
     quads = groups // 2
     quad = (own, chans, BLOCK)
-    keep, send = call(
-        cross_kernel,
-        (shape((2, 2, *quad), f32), shape((2, 2, *quad), bf16)),
-        spec,
-        lag_back,
-        turn,
-        middle,
-        scratch=[(half * chans, BLOCK)],
-        flops=2 * work,
-        name="cross",
-    )
+    vmem = pl.BlockSpec(memory_space=pltpu.VMEM)
+    carried, keep, send = pl.pallas_call(
+        transform_kernel,
+        out_shape=(pieces, shape((2, 2, *quad), f32), shape((2, 2, *quad), bf16)),
+        in_specs=[vmem] * 7,
+        out_specs=(pl.BlockSpec(memory_space=pltpu.HBM), vmem, vmem),
+        scratch_shapes=[
+            pltpu.VMEM((both * half, 2 * BLOCK), f32),
+            pltpu.VMEM((half * both, BLOCK), f32),
+            pltpu.VMEM((half * chans, BLOCK), f32),
+            pltpu.VMEM((half, both, BLOCK), bf16),
+            pltpu.SemaphoreType.DMA(()),
+        ],
+        compiler_params=pltpu.CompilerParams(vmem_limit_bytes=40 * 2**20),
+        cost_estimate=pl.CostEstimate(flops=6 * work, bytes_accessed=2**21, transcendentals=0),
+        name="transform",
+    )(here, filter_spec, forward, back, lag_back, turn, middle)
     other = lax.ppermute(send, "dp", [(i, i ^ 2) for i in range(groups)])
-    carried = call(
-        conv_kernel,
-        pieces,
-        spec,
-        filter_spec,
-        back,
-        turn,
-        middle,
-        send,
-        scratch=[(half * both, BLOCK)],
-        flops=4 * work,
-        any_space=1,
-        name="conv",
-    )
     keep, send = call(
         core_kernel,
         (shape((2, *quad), f32), shape((2, *quad), bf16)),

time: 59.8 us -> 59 us (0.987)
  Pallas kernels: 5.88 us -> 5.1 us
    pallas_call x7 -> x4, Pallas kernels: 4 us -> 1.39 us  [call(): pl.pallas_call(kernel, out_shape=out, in_specs=[vmem] * (len(args) - any_...]
    pallas_call x0 -> x1, Pallas kernels: none -> 1.82 us  [local(): pl.pallas_call(transform_kernel, out_shape=(pieces, shape((2, 2, *quad),...]
  transfers between devices with their start and end apart: 3 -> 3, of which waited for: 1 -> 1; matrix products, arithmetic and copies ran while one was open for 0% -> 0% of each run, Pallas kernels for 3% -> 1%
where the time goes in v6:
time: 59 us; the launch traced here: 58.7 us
  starting transfers between devices  38.1 us (65%)
  blocking collectives  8.81 us (15%)
  waiting for transfers between devices  5.75 us (10%)
  Pallas kernels  5.1 us (9%)
  between operations  0.81 us (1%)
    all_to_all x1, starting transfers between devices, local(): lax.all_to_all(gated, 'ctx', 0, 0, tiled=True, axis_index_groups=[slots(h...  20.4 us
    all_to_all x1, starting transfers between devices, local(): lax.all_to_all(carried, 'ctx', 0, 0, tiled=True, axis_index_groups=[slots...  14.6 us
    all_to_all x1, waiting for transfers between devices, local(): lax.all_to_all(gated, 'ctx', 0, 0, tiled=True, axis_index_groups=[slots(h...  5.74 us
    all_gather x1, blocking collectives, local(): other = lax.all_gather(send, 'dp', axis=0, axis_index_groups=sides)  4.59 us
    all_gather x1, blocking collectives, local(): other = lax.all_gather(send, 'dp', axis=0, axis_index_groups=cores)  4.23 us
    ppermute x1, starting transfers between devices, local(): other = lax.ppermute(send, 'dp', [(i, i ^ 2) for i in range(groups)])  3.1 us
    pallas_call x1, Pallas kernels, local(): pl.pallas_call(gate_kernel, out_shape=pieces, in_specs=[pl.BlockSpec(memo...  1.89 us
    pallas_call x1, Pallas kernels, local(): pl.pallas_call(transform_kernel, out_shape=(pieces, shape((2, 2, *quad),...  1.82 us
  transfers between devices with their start and end apart: 3, of which 1 were waited for; matrix products, arithmetic and copies ran while one was open for 0% of the time, Pallas kernels for 1%

profile of v6, /device:TPU:1, one launch (start us, length us, event | category | flops | bytes accessed | tf_op | source)
XLA Modules:
  0.0 58.7 jit_solution(15749095108308842973)
XLA Ops:
  0.6 0.0 copy-start.4
  0.6 1.9 %gate.1 = bf16[64,16,128]{2,1,0:T(8,128)(2,1)} custom-call(bf16[512,128]{1,0:T(8,128)(2,1)} %bitcast.9, bf16[512,128]{1,0:T(8,128)(2,1)} %bitcast.11, bf16[512,128]{1,0:T(8,128)(2,1)} %bitcast.13, bf16[512,128]{1,0:T(8,128)(2,1)} %bitcast.17), custom_call_target="tpu_custom_call" | custom-call | flops 131072 | bytes 786432 | tf_op jit(solution)/shard_map/gate/pallas_call | solution.py:269
  2.5 0.0 copy-start.3
  2.6 0.0 copy-start.5
  2.6 0.0 copy-start.6
  2.6 20.4 %all-to-all-start = ((bf16[64,16,128]{2,1,0:T(8,128)(2,1)}), bf16[64,16,128]{2,1,0:T(8,128)(2,1)S(1)}, u32[]{:S(2)}, u32[]{:S(2)}) async-start(bf16[64,16,128]{2,1,0:T(8,128)(2,1)} %gate.1), calls=%async_computation | async-start | bytes 524288 | tf_op jit(solution)/shard_map/all_to_all | solution.py:284
  23.0 0.0 copy-done.4
  23.0 0.0 copy-done.3
  23.1 0.0 copy-done.5
  23.1 0.0 copy-done.6
  23.1 0.0 copy-start.7
  23.1 0.0 copy-start.8
  23.1 0.6 filter.1.filter_ref
  23.7 5.7 %all-to-all-done.both_ref = bf16[64,16,128]{2,1,0:T(8,128)(2,1)S(1)} async-done(((bf16[64,16,128]{2,1,0:T(8,128)(2,1)}), bf16[64,16,128]{2,1,0:T(8,128)(2,1)S(1)}, u32[]{:S(2)}, u32[]{:S(2)}) %all-to-all-start) | async-done | bytes 262176 | tf_op jit(solution)/shard_map/all_to_all | solution.py:284
  29.4 0.0 copy-done.7
  29.4 0.0 copy-done.8
  29.4 1.8 %transform.1 = (bf16[64,16,128]{2,1,0:T(8,128)(2,1)}, f32[2,2,8,8,128]{4,3,2,1,0:T(8,128)S(1)}, bf16[2,2,8,8,128]{4,3,2,1,0:T(8,128)(2,1)S(1)}) custom-call(bf16[64,16,128]{2,1,0:T(8,128)(2,1)S(1)} %all-to-all-done.both_ref, f32[512,256]{1,0:T(8,128)S(1)} %filter.1.filter_ref, bf16[128,192]{1,0:T(8,128)(2,1)S(1)} %copy-done.6, ...), custom_call_target="tpu_custom_call" | custom-call | flops 1207959552 | bytes 2097152 | tf_op jit(solution)/shard_map/transform/pallas_call | solution.py:302
  31.2 3.1 %collective-permute-start = (bf16[2,2,8,8,128]{4,3,2,1,0:T(8,128)(2,1)S(1)}, bf16[2,2,8,8,128]{4,3,2,1,0:T(8,128)(2,1)S(1)}, u32[]{:S(2)}, u32[]{:S(2)}) collective-permute-start(bf16[2,2,8,8,128]{4,3,2,1,0:T(8,128)(2,1)S(1)} %get-tuple-element.17), channel_id=1, source_target_pairs={{0,128},{64,192},{128,0},{192,64},{256,384},{320,448},{384,256},{4... | collective-permute-start | bytes 196616 | tf_op jit(solution)/shard_map/ppermute | solution.py:318
  34.4 14.6 %all-to-all-start.1 = ((bf16[64,16,128]{2,1,0:T(8,128)(2,1)}), bf16[64,16,128]{2,1,0:T(8,128)(2,1)S(1)}, u32[]{:S(2)}, u32[]{:S(2)}) async-start(bf16[64,16,128]{2,1,0:T(8,128)(2,1)} %get-tuple-element.15), calls=%async_computation.1 | async-start | bytes 524288 | tf_op jit(solution)/shard_map/all_to_all | solution.py:338
  49.0 0.0 collective-permute-done.other_ref
  49.0 0.0 copy-start.2
  49.0 0.0 copy-start
  49.0 0.0 copy-start.1
  49.0 4.2 %all-gather = bf16[4,8,8,128]{3,2,1,0:T(8,128)(2,1)S(1)} all-gather(bf16[2,8,8,128]{3,2,1,0:T(8,128)(2,1)S(1)} %get-tuple-element.19), channel_id=2, replica_groups={{0,64},{128,192},{256,320},{384,448},{1,65},{129,193},{257,321},{385,44..., dimensions={0}, use_global_device_ids=true | all-gather | bytes 98304 | tf_op jit(solution)/shard_map/all_gather | solution.py:328
  53.3 4.6 %all-gather.1 = bf16[16,8,128]{2,1,0:T(8,128)(2,1)S(1)} all-gather(bf16[8,8,128]{2,1,0:T(8,128)(2,1)S(1)} %get-tuple-element.21), channel_id=3, replica_groups={{0,256},{64,320},{128,384},{192,448},{1,257},{65,321},{129,385},{193,44..., dimensions={0}, use_global_device_ids=true | all-gather | bytes 49152 | tf_op jit(solution)/shard_map/all_gather | solution.py:337
  57.9 0.0 all-to-all-done.1.both_ref
  57.9 0.0 copy-done.2
  57.9 0.0 copy-done
  57.9 0.0 copy-done.1
  57.9 0.8 %final.1 = (bf16[512,128]{1,0:T(8,128)(2,1)}, bf16[512,128]{1,0:T(8,128)(2,1)}, bf16[512,128]{1,0:T(8,128)(2,1)}, f32[8,1024]{1,0:T(8,128)}) custom-call(bf16[64,16,128]{2,1,0:T(8,128)(2,1)S(1)} %all-to-all-done.1.both_ref, bf16[512,128]{1,0:T(8,128)(2,1)S(1)} %bitcast.10, bf16[512,128]{1,0:T(8,128)(2,1)S(1)} %bitcast.12, bf16[512,128]{1,0:T(8,128)(2,1)S(1)} %bitcast.14, ...), custom_call_target="tpu_custom_call" | custom-call | bytes 720896 | tf_op jit(solution)/shard_map/final/pallas_call | solution.py:240
  (2 shorter events, 0.0 us)
Async XLA Ops:
  0.6 22.4 %copy-start.4 = (bf16[768,256]{1,0:T(8,128)(2,1)S(1)}, bf16[768,256]{1,0:T(8,128)(2,1)}, u32[]{:S(2)}) copy-start(bf16[768,256]{1,0:T(8,128)(2,1)} %constant.13.clone.middle_ref) | copy-start | bytes 1179652
  2.5 20.5 %copy-start.3 = (f32[8,8192]{1,0:T(8,128)S(1)}, f32[8,8192]{1,0:T(8,128)}, u32[]{:S(2)}) copy-start(f32[8,8192]{1,0:T(8,128)} %filter_ref.1) | copy-start | bytes 786436
  2.6 20.5 %copy-start.5 = (f32[2,64,128]{2,1,0:T(8,128)S(1)}, f32[2,64,128]{2,1,0:T(8,128)}, u32[]{:S(2)}) copy-start(f32[2,64,128]{2,1,0:T(8,128)} %constant.14.clone.turn_ref) | copy-start | bytes 196612
  2.6 20.5 %copy-start.6 = (bf16[128,192]{1,0:T(8,128)(2,1)S(1)}, bf16[128,192]{1,0:T(8,128)(2,1)}, u32[]{:S(2)}) copy-start(bf16[128,192]{1,0:T(8,128)(2,1)} %constant.10.clone.forward_ref) | copy-start | bytes 147460
  2.6 26.8 %all-to-all-start = ((bf16[64,16,128]{2,1,0:T(8,128)(2,1)}), bf16[64,16,128]{2,1,0:T(8,128)(2,1)S(1)}, u32[]{:S(2)}, u32[]{:S(2)}) async-start(bf16[64,16,128]{2,1,0:T(8,128)(2,1)} %gate.1), calls=%async_computation | async-start | bytes 524288 | tf_op jit(solution)/shard_map/all_to_all | solution.py:284
  23.1 6.3 %copy-start.7 = (bf16[64,128]{1,0:T(8,128)(2,1)S(1)}, bf16[64,128]{1,0:T(8,128)(2,1)}, u32[]{:S(2)}) copy-start(bf16[64,128]{1,0:T(8,128)(2,1)} %constant.12.clone.lag_ref) | copy-start | bytes 49156
  23.1 6.3 %copy-start.8 = (bf16[64,128]{1,0:T(8,128)(2,1)S(1)}, bf16[64,128]{1,0:T(8,128)(2,1)}, u32[]{:S(2)}) copy-start(bf16[64,128]{1,0:T(8,128)(2,1)} %constant.11.clone.back_ref) | copy-start | bytes 49156
  31.2 17.7 %collective-permute-start = (bf16[2,2,8,8,128]{4,3,2,1,0:T(8,128)(2,1)S(1)}, bf16[2,2,8,8,128]{4,3,2,1,0:T(8,128)(2,1)S(1)}, u32[]{:S(2)}, u32[]{:S(2)}) collective-permute-start(bf16[2,2,8,8,128]{4,3,2,1,0:T(8,128)(2,1)S(1)} %get-tuple-element.17), channel_id=1, source_target_pairs={{0,128},{64,192},{128,0},{192,64},{256,384},{320,448},{384,256},{4... | collective-permute-start | bytes 196616 | tf_op jit(solution)/shard_map/ppermute | solution.py:318
  34.4 23.5 %all-to-all-start.1 = ((bf16[64,16,128]{2,1,0:T(8,128)(2,1)}), bf16[64,16,128]{2,1,0:T(8,128)(2,1)S(1)}, u32[]{:S(2)}, u32[]{:S(2)}) async-start(bf16[64,16,128]{2,1,0:T(8,128)(2,1)} %get-tuple-element.15), calls=%async_computation.1 | async-start | bytes 524288 | tf_op jit(solution)/shard_map/all_to_all | solution.py:338
  49.0 8.9 %copy-start.2 = (bf16[1,512,128]{2,1,0:T(8,128)(2,1)S(1)}, bf16[1,512,128]{2,1,0:T(8,128)(2,1)}, u32[]{:S(2)}) copy-start(bf16[1,512,128]{2,1,0:T(8,128)(2,1)} %param.13) | copy-start | bytes 393220
  49.0 8.9 %copy-start = (bf16[1,512,128]{2,1,0:T(8,128)(2,1)S(1)}, bf16[1,512,128]{2,1,0:T(8,128)(2,1)}, u32[]{:S(2)}) copy-start(bf16[1,512,128]{2,1,0:T(8,128)(2,1)} %param.11) | copy-start | bytes 393220
  49.0 8.9 %copy-start.1 = (bf16[1,512,128]{2,1,0:T(8,128)(2,1)S(1)}, bf16[1,512,128]{2,1,0:T(8,128)(2,1)}, u32[]{:S(2)}) copy-start(bf16[1,512,128]{2,1,0:T(8,128)(2,1)} %param.12) | copy-start | bytes 393220

commit v7 on v6

--- a/solution.py
+++ b/solution.py
@@ -50,6 +50,7 @@
     mid_high, mid_low = split_table(np.block([[cos, -sin], [sin, cos]]))
     return {
         "forward": np.concatenate([first_high, first_high, first_low], 1),
+        "exact": np.concatenate([first_high, first_low], 1),
         "back": back[slots(half, FAR_OUT)],
         "lag": back,
         "middle": np.concatenate([mid_high, mid_high, mid_low], 0),
@@ -75,8 +76,7 @@
     cols = jnp.concatenate([rows_ref[pl.ds(c, half, stride=chans), :] for c in range(chans)], 1)
     if exact:
         high = cols.astype(bf16)
-        table = jnp.concatenate([forward_ref[:, :half], forward_ref[:, 2 * half :]], 1)
-        section = dot(table, jnp.concatenate([high, high], 0))
+        section = dot(forward_ref[...], jnp.concatenate([high, high], 0))
     else:
         high, low = split(cols)
         section = dot(forward_ref[...], jnp.concatenate([high, low, high], 0))
@@ -199,11 +199,17 @@
     inverse_rows(
         jnp.concatenate([conv, dkv], 0), both, half, out_rows, back_ref, turn_ref, middle_ref
     )
-    made[...] = out_rows[...].reshape(half, both, BLOCK).astype(bf16)
-    done = pltpu.make_async_copy(made, out_hbm, sem)
-    done.start()
+    sent = []
+    part = half // 2
+    for p in range(2):
+        span = pl.ds(p * part, part)
+        rows = out_rows[p * part * both : (p + 1) * part * both, :]
+        made[span] = rows.reshape(part, both, BLOCK).astype(bf16)
+        sent.append(pltpu.make_async_copy(made.at[span], out_hbm.at[span], sem.at[p]))
+        sent[p].start()
     cross_terms(spec_ref, lag_ref, turn_ref, middle_ref, keep_ref, send_ref, lag_rows)
-    done.wait()
+    for done in sent:
+        done.wait()
 
 
 def final_kernel(
@@ -309,12 +315,12 @@
             pltpu.VMEM((half * both, BLOCK), f32),
             pltpu.VMEM((half * chans, BLOCK), f32),
             pltpu.VMEM((half, both, BLOCK), bf16),
-            pltpu.SemaphoreType.DMA(()),
+            pltpu.SemaphoreType.DMA((2,)),
         ],
         compiler_params=pltpu.CompilerParams(vmem_limit_bytes=40 * 2**20),
         cost_estimate=pl.CostEstimate(flops=6 * work, bytes_accessed=2**21, transcendentals=0),
         name="transform",
-    )(here, filter_spec, forward, back, lag_back, turn, middle)
+    )(here, filter_spec, tables["exact"], back, lag_back, turn, middle)
     other = lax.ppermute(send, "dp", [(i, i ^ 2) for i in range(groups)])
     keep, send = call(
         core_kernel,

time: 59 us -> 58.9 us (level)
  no operation moved by 1% of the time
where the time goes in v7:
time: 58.9 us; the launch traced here: 58.6 us
  starting transfers between devices  38.1 us (65%)
  blocking collectives  8.82 us (15%)
  waiting for transfers between devices  5.74 us (10%)
  Pallas kernels  5.06 us (9%)
  between operations  0.82 us (1%)
    all_to_all x1, starting transfers between devices, local(): lax.all_to_all(gated, 'ctx', 0, 0, tiled=True, axis_index_groups=[slots(h...  20.4 us
    all_to_all x1, starting transfers between devices, local(): lax.all_to_all(carried, 'ctx', 0, 0, tiled=True, axis_index_groups=[slots...  14.6 us
    all_to_all x1, waiting for transfers between devices, local(): lax.all_to_all(gated, 'ctx', 0, 0, tiled=True, axis_index_groups=[slots(h...  5.73 us
    all_gather x1, blocking collectives, local(): other = lax.all_gather(send, 'dp', axis=0, axis_index_groups=sides)  4.59 us
    all_gather x1, blocking collectives, local(): other = lax.all_gather(send, 'dp', axis=0, axis_index_groups=cores)  4.23 us
    ppermute x1, starting transfers between devices, local(): other = lax.ppermute(send, 'dp', [(i, i ^ 2) for i in range(groups)])  3.1 us
    pallas_call x1, Pallas kernels, local(): pl.pallas_call(gate_kernel, out_shape=pieces, in_specs=[pl.BlockSpec(memo...  1.91 us
    pallas_call x1, Pallas kernels, local(): pl.pallas_call(transform_kernel, out_shape=(pieces, shape((2, 2, *quad),...  1.76 us
  transfers between devices with their start and end apart: 3, of which 1 were waited for; matrix products, arithmetic and copies ran while one was open for 0% of the time, Pallas kernels for 1%

profile of v7, /device:TPU:1, one launch (start us, length us, event | category | flops | bytes accessed | tf_op | source)
XLA Modules:
  0.0 58.6 jit_solution(16125530108259865933)
XLA Ops:
  0.6 0.0 copy-start.4
  0.6 1.9 %gate.1 = bf16[64,16,128]{2,1,0:T(8,128)(2,1)} custom-call(bf16[512,128]{1,0:T(8,128)(2,1)} %bitcast.9, bf16[512,128]{1,0:T(8,128)(2,1)} %bitcast.11, bf16[512,128]{1,0:T(8,128)(2,1)} %bitcast.13, bf16[512,128]{1,0:T(8,128)(2,1)} %bitcast.17), custom_call_target="tpu_custom_call" | custom-call | flops 131072 | bytes 786432 | tf_op jit(solution)/shard_map/gate/pallas_call | solution.py:275
  2.6 0.0 copy-start.3
  2.6 0.0 copy-start.5
  2.6 0.0 copy-start.6
  2.6 20.4 %all-to-all-start = ((bf16[64,16,128]{2,1,0:T(8,128)(2,1)}), bf16[64,16,128]{2,1,0:T(8,128)(2,1)S(1)}, u32[]{:S(2)}, u32[]{:S(2)}) async-start(bf16[64,16,128]{2,1,0:T(8,128)(2,1)} %gate.1), calls=%async_computation | async-start | bytes 524288 | tf_op jit(solution)/shard_map/all_to_all | solution.py:290
  23.1 0.0 copy-done.4
  23.1 0.0 copy-done.3
  23.1 0.0 copy-done.5
  23.1 0.0 copy-done.6
  23.1 0.0 copy-start.7
  23.1 0.0 copy-start.8
  23.1 0.0 copy-start.9
  23.1 0.6 filter.1.filter_ref
  23.7 5.7 %all-to-all-done.both_ref = bf16[64,16,128]{2,1,0:T(8,128)(2,1)S(1)} async-done(((bf16[64,16,128]{2,1,0:T(8,128)(2,1)}), bf16[64,16,128]{2,1,0:T(8,128)(2,1)S(1)}, u32[]{:S(2)}, u32[]{:S(2)}) %all-to-all-start) | async-done | bytes 262176 | tf_op jit(solution)/shard_map/all_to_all | solution.py:290
  29.4 0.0 copy-done.7
  29.4 0.0 copy-done.8
  29.4 0.0 copy-done.9
  29.4 1.8 %transform.1 = (bf16[64,16,128]{2,1,0:T(8,128)(2,1)}, f32[2,2,8,8,128]{4,3,2,1,0:T(8,128)S(1)}, bf16[2,2,8,8,128]{4,3,2,1,0:T(8,128)(2,1)S(1)}) custom-call(bf16[64,16,128]{2,1,0:T(8,128)(2,1)S(1)} %all-to-all-done.both_ref, f32[512,256]{1,0:T(8,128)S(1)} %filter.1.filter_ref, bf16[128,128]{1,0:T(8,128)(2,1)S(1)} %copy-done.7, ...), custom_call_target="tpu_custom_call" | custom-call | flops 1207959552 | bytes 2097152 | tf_op jit(solution)/shard_map/transform/pallas_call | solution.py:308
  31.2 3.1 %collective-permute-start = (bf16[2,2,8,8,128]{4,3,2,1,0:T(8,128)(2,1)S(1)}, bf16[2,2,8,8,128]{4,3,2,1,0:T(8,128)(2,1)S(1)}, u32[]{:S(2)}, u32[]{:S(2)}) collective-permute-start(bf16[2,2,8,8,128]{4,3,2,1,0:T(8,128)(2,1)S(1)} %get-tuple-element.17), channel_id=1, source_target_pairs={{0,128},{64,192},{128,0},{192,64},{256,384},{320,448},{384,256},{4... | collective-permute-start | bytes 196616 | tf_op jit(solution)/shard_map/ppermute | solution.py:324
  34.3 14.6 %all-to-all-start.1 = ((bf16[64,16,128]{2,1,0:T(8,128)(2,1)}), bf16[64,16,128]{2,1,0:T(8,128)(2,1)S(1)}, u32[]{:S(2)}, u32[]{:S(2)}) async-start(bf16[64,16,128]{2,1,0:T(8,128)(2,1)} %get-tuple-element.15), calls=%async_computation.1 | async-start | bytes 524288 | tf_op jit(solution)/shard_map/all_to_all | solution.py:344
  48.9 0.0 collective-permute-done.other_ref
  48.9 0.0 copy-start.2
  49.0 0.0 copy-start
  49.0 0.0 copy-start.1
  49.0 4.2 %all-gather = bf16[4,8,8,128]{3,2,1,0:T(8,128)(2,1)S(1)} all-gather(bf16[2,8,8,128]{3,2,1,0:T(8,128)(2,1)S(1)} %get-tuple-element.19), channel_id=2, replica_groups={{0,64},{128,192},{256,320},{384,448},{1,65},{129,193},{257,321},{385,44..., dimensions={0}, use_global_device_ids=true | all-gather | bytes 98304 | tf_op jit(solution)/shard_map/all_gather | solution.py:334
  53.2 4.6 %all-gather.1 = bf16[16,8,128]{2,1,0:T(8,128)(2,1)S(1)} all-gather(bf16[8,8,128]{2,1,0:T(8,128)(2,1)S(1)} %get-tuple-element.21), channel_id=3, replica_groups={{0,256},{64,320},{128,384},{192,448},{1,257},{65,321},{129,385},{193,44..., dimensions={0}, use_global_device_ids=true | all-gather | bytes 49152 | tf_op jit(solution)/shard_map/all_gather | solution.py:343
  57.8 0.0 all-to-all-done.1.both_ref
  57.8 0.0 copy-done.2
  57.8 0.0 copy-done
  57.8 0.0 copy-done.1
  57.8 0.8 %final.1 = (bf16[512,128]{1,0:T(8,128)(2,1)}, bf16[512,128]{1,0:T(8,128)(2,1)}, bf16[512,128]{1,0:T(8,128)(2,1)}, f32[8,1024]{1,0:T(8,128)}) custom-call(bf16[64,16,128]{2,1,0:T(8,128)(2,1)S(1)} %all-to-all-done.1.both_ref, bf16[512,128]{1,0:T(8,128)(2,1)S(1)} %bitcast.10, bf16[512,128]{1,0:T(8,128)(2,1)S(1)} %bitcast.12, bf16[512,128]{1,0:T(8,128)(2,1)S(1)} %bitcast.14, ...), custom_call_target="tpu_custom_call" | custom-call | bytes 720896 | tf_op jit(solution)/shard_map/final/pallas_call | solution.py:246
  (2 shorter events, 0.0 us)
Async XLA Ops:
  0.6 22.4 %copy-start.4 = (bf16[768,256]{1,0:T(8,128)(2,1)S(1)}, bf16[768,256]{1,0:T(8,128)(2,1)}, u32[]{:S(2)}) copy-start(bf16[768,256]{1,0:T(8,128)(2,1)} %constant.16.clone.middle_ref) | copy-start | bytes 1179652
  2.6 20.5 %copy-start.3 = (f32[8,8192]{1,0:T(8,128)S(1)}, f32[8,8192]{1,0:T(8,128)}, u32[]{:S(2)}) copy-start(f32[8,8192]{1,0:T(8,128)} %filter_ref.1) | copy-start | bytes 786436
  2.6 20.5 %copy-start.5 = (f32[2,64,128]{2,1,0:T(8,128)S(1)}, f32[2,64,128]{2,1,0:T(8,128)}, u32[]{:S(2)}) copy-start(f32[2,64,128]{2,1,0:T(8,128)} %constant.17.clone.turn_ref) | copy-start | bytes 196612
  2.6 20.5 %copy-start.6 = (bf16[128,192]{1,0:T(8,128)(2,1)S(1)}, bf16[128,192]{1,0:T(8,128)(2,1)}, u32[]{:S(2)}) copy-start(bf16[128,192]{1,0:T(8,128)(2,1)} %constant.12.clone.forward_ref) | copy-start | bytes 147460
  2.6 26.8 %all-to-all-start = ((bf16[64,16,128]{2,1,0:T(8,128)(2,1)}), bf16[64,16,128]{2,1,0:T(8,128)(2,1)S(1)}, u32[]{:S(2)}, u32[]{:S(2)}) async-start(bf16[64,16,128]{2,1,0:T(8,128)(2,1)} %gate.1), calls=%async_computation | async-start | bytes 524288 | tf_op jit(solution)/shard_map/all_to_all | solution.py:290
  23.1 6.3 %copy-start.7 = (bf16[128,128]{1,0:T(8,128)(2,1)S(1)}, bf16[128,128]{1,0:T(8,128)(2,1)}, u32[]{:S(2)}) copy-start(bf16[128,128]{1,0:T(8,128)(2,1)} %constant.13.clone.forward_ref) | copy-start | bytes 98308
  23.1 6.3 %copy-start.8 = (bf16[64,128]{1,0:T(8,128)(2,1)S(1)}, bf16[64,128]{1,0:T(8,128)(2,1)}, u32[]{:S(2)}) copy-start(bf16[64,128]{1,0:T(8,128)(2,1)} %constant.15.clone.lag_ref) | copy-start | bytes 49156
  23.1 6.3 %copy-start.9 = (bf16[64,128]{1,0:T(8,128)(2,1)S(1)}, bf16[64,128]{1,0:T(8,128)(2,1)}, u32[]{:S(2)}) copy-start(bf16[64,128]{1,0:T(8,128)(2,1)} %constant.14.clone.back_ref) | copy-start | bytes 49156
  31.2 17.7 %collective-permute-start = (bf16[2,2,8,8,128]{4,3,2,1,0:T(8,128)(2,1)S(1)}, bf16[2,2,8,8,128]{4,3,2,1,0:T(8,128)(2,1)S(1)}, u32[]{:S(2)}, u32[]{:S(2)}) collective-permute-start(bf16[2,2,8,8,128]{4,3,2,1,0:T(8,128)(2,1)S(1)} %get-tuple-element.17), channel_id=1, source_target_pairs={{0,128},{64,192},{128,0},{192,64},{256,384},{320,448},{384,256},{4... | collective-permute-start | bytes 196616 | tf_op jit(solution)/shard_map/ppermute | solution.py:324
  34.3 23.5 %all-to-all-start.1 = ((bf16[64,16,128]{2,1,0:T(8,128)(2,1)}), bf16[64,16,128]{2,1,0:T(8,128)(2,1)S(1)}, u32[]{:S(2)}, u32[]{:S(2)}) async-start(bf16[64,16,128]{2,1,0:T(8,128)(2,1)} %get-tuple-element.15), calls=%async_computation.1 | async-start | bytes 524288 | tf_op jit(solution)/shard_map/all_to_all | solution.py:344
  48.9 8.9 %copy-start.2 = (bf16[1,512,128]{2,1,0:T(8,128)(2,1)S(1)}, bf16[1,512,128]{2,1,0:T(8,128)(2,1)}, u32[]{:S(2)}) copy-start(bf16[1,512,128]{2,1,0:T(8,128)(2,1)} %param.14) | copy-start | bytes 393220
  49.0 8.9 %copy-start = (bf16[1,512,128]{2,1,0:T(8,128)(2,1)S(1)}, bf16[1,512,128]{2,1,0:T(8,128)(2,1)}, u32[]{:S(2)}) copy-start(bf16[1,512,128]{2,1,0:T(8,128)(2,1)} %param.12) | copy-start | bytes 393220
  49.0 8.9 %copy-start.1 = (bf16[1,512,128]{2,1,0:T(8,128)(2,1)S(1)}, bf16[1,512,128]{2,1,0:T(8,128)(2,1)}, u32[]{:S(2)}) copy-start(bf16[1,512,128]{2,1,0:T(8,128)(2,1)} %param.13) | copy-start | bytes 393220
